TPU v7x, 256 devices: a whole 4x4x8 slice. The times are simulated.
256 devices in a mesh: coal: 8 (over z_lo, core), section: 4 (over y), tensor: 8 (over x, z_hi).
Axes of the slice: x: 4, y: 4, z: 8 (z_hi: 2, z_lo: 4; z = z_hi * 4 + z_lo), core: 2. Of those that a mesh axis runs over, the one named last changes fastest.
Arguments:
- hidden: bfloat16 [32, 128, 8192], P('coal', None, 'section'), parts along dimension 0, may hold values from -120 to 120
- norm_gain: float32 [8192], P('section'), may hold values from 0.1 to 1.9
- w_query: bfloat16 [8192, 8192], P('section', 'tensor'), may hold values from -0.0625 to 0.0625
- w_key: bfloat16 [8192, 1024], P('section', 'tensor'), may hold values from -0.0625 to 0.0625
- w_value: bfloat16 [8192, 1024], P('section', 'tensor'), may hold values from -0.0625 to 0.0625
- w_out: bfloat16 [8192, 8192], P('tensor', 'section'), may hold values from -0.0625 to 0.0625
- cache_key: bfloat16 [8192, 1024], P('section', 'tensor'), may hold values from -400 to 400
- cache_value: bfloat16 [8192, 1024], P('section', 'tensor'), may hold values from -6 to 6
- block_mask: int32 [32, 128], P('coal'), parts along dimension 0, may hold values from 0 to 1
Outputs:
- attn_out: bfloat16 [32, 128, 8192], P('coal', None, ('section', 'tensor')), parts along dimension 0
There are 8 independent parts, one for each index of `coal`. A program takes and returns all parts, laid end to end along the dimension named above; an argument that names none is the same for every part. Nothing has to cross between parts.
All inputs are finite; a program needn't handle non-finite values.
Results may differ from a plain program's by a relative error of at most 0.015.
Values may be sent and summed in bfloat16 or wider, within the bound.
No kernel may reach another device: no remote copies, remote signals or barrier semaphores. Data moves between devices by JAX's collectives and lax.ppermute only.
A program may use at most 128 MiB of HBM per device.

v0:
```python
import functools
import math

import jax
import jax.numpy as jnp
from jax import lax
from jax.experimental import pallas as pl
from jax.experimental.pallas import tpu as pltpu
from jax.sharding import PartitionSpec as P

D = 8192
HD = 128
NBLK = 128
BLOCK = 64
rope_base = 500000.0
norm_eps = 1e-05
masked_score = -1e30
BF = jnp.bfloat16
F32 = jnp.float32
HALVES = 2
TILE = 1024
ANSWER = 128
MIB = 1024 * 1024


def section_shift(x, by):
    n = lax.axis_size("section")
    return lax.ppermute(x, "section", [(i, (i + by) % n) for i in range(n)])


def x_shift(x, by):
    n = lax.axis_size("tensor") // 2
    return lax.ppermute(
        x, "tensor", [(i, ((i // 2 + by) % n) * 2 + i % 2) for i in range(2 * n)]
    )


def z_swap(x):
    return lax.ppermute(x, "tensor", [(i, i ^ 1) for i in range(lax.axis_size("tensor"))])


def core_swap(x):
    return lax.ppermute(x, "coal", [(i, i ^ 1) for i in range(lax.axis_size("coal"))])


def project_kernel(place, hidden, gain, w_query, w_key, w_value, *rest):
    outs, (rows, weights, scaled, product, sem) = rest[:-5], rest[-5:]
    count, answer, width = hidden.shape
    queries = w_query.shape[1]
    steps, _, _, depth = rows.shape
    copies = []
    for k in range(steps):
        at = pl.ds(k * depth, depth)
        group = [
            (hidden.at[lax.rem(place[0] + r, count), :, at], rows.at[k, r]) for r in range(count)
        ]
        group += [
            (w_query.at[at], weights.at[at, pl.ds(0, queries)]),
            (w_key.at[at], weights.at[at, pl.ds(queries, HD)]),
            (w_value.at[at], weights.at[at, pl.ds(queries + HD, HD)]),
        ]
        copies.append(
            [pltpu.make_async_copy(a, b, sem.at[k, i]) for i, (a, b) in enumerate(group)]
        )
        for copy in copies[-1]:
            copy.start()

    squares = [jnp.zeros((answer, 128), F32) for _ in range(count)]
    for k in range(steps):
        at = slice(k * depth, (k + 1) * depth)
        for copy in copies[k]:
            copy.wait()
        for r in range(count):
            x = rows[k, r].astype(F32)
            x2 = x * x
            for j in range(depth // 128):
                squares[r] = squares[r] + x2[:, j * 128 : (j + 1) * 128]
            scaled[k, r * answer : (r + 1) * answer] = (x * gain[:, at]).astype(BF)
        partial = jnp.dot(scaled[k], weights[at], preferred_element_type=F32)
        if k == 0:
            product[...] = partial
        elif k < steps - 1:
            product[...] += partial
        else:
            partial = product[...] + partial
            lane = lax.broadcasted_iota(jnp.int32, (answer, 128), 1)
            for r in range(count):
                total = jnp.sum(squares[r], axis=-1, keepdims=True)
                high = total.astype(BF).astype(F32)
                pair = jnp.where(lane == 0, high, jnp.where(lane == 1, total - high, 0.0))
                out = outs[r]
                out[:, : queries + 2 * HD] = partial[r * answer : (r + 1) * answer].astype(BF)
                out[:, queries + 2 * HD :] = pair.astype(BF)


def project(place, hidden, gain, w_query, w_key, w_value):
    count, answer, width = hidden.shape
    total = w_query.shape[1] + 2 * HD
    steps = 4
    smem = pl.BlockSpec(memory_space=pltpu.SMEM)
    vmem = pl.BlockSpec(memory_space=pltpu.VMEM)
    anywhere = pl.BlockSpec(memory_space=pl.ANY)
    return pl.pallas_call(
        project_kernel,
        in_specs=[smem, anywhere, vmem, anywhere, anywhere, anywhere],
        out_specs=[vmem] * count,
        out_shape=[jax.ShapeDtypeStruct((answer, total + HD), BF)] * count,
        scratch_shapes=[
            pltpu.VMEM((steps, count, answer, width // steps), BF),
            pltpu.VMEM((width, total), BF),
            pltpu.VMEM((steps, count * answer, width // steps), BF),
            pltpu.VMEM((count * answer, total), F32),
            pltpu.SemaphoreType.DMA((steps, count + 3)),
        ],
        compiler_params=pltpu.CompilerParams(vmem_limit_bytes=60 * MIB),
        cost_estimate=pl.CostEstimate(
            flops=2 * count * answer * width * total, bytes_accessed=9 * MIB, transcendentals=0
        ),
        name="project",
    )(place, hidden, gain, w_query, w_key, w_value)


def rotate_kernel(place, p0, p1, p2, p3, cosine, sine, cache_key, cache_value, before1, before3,
                  queries, near_key, near_value, piece, sem):
    size = piece.shape[1]
    at = pl.ds(pl.multiple_of(place[1] * size, size), size)
    copies = [
        pltpu.make_async_copy(cache.at[at], piece.at[i], sem.at[i])
        for i, cache in enumerate((cache_key, cache_value))
    ]
    for copy in copies:
        copy.start()
    answer = p0.shape[0]
    span = answer // HALVES
    heads = queries.shape[0] // answer
    width = (heads + 2) * HD
    total = (
        p0[:, width:].astype(F32) + p1[:, width:].astype(F32)
        + p2[:, width:].astype(F32) + p3[:, width:].astype(F32)
    )
    scale = lax.rsqrt((total[:, 0:1] + total[:, 1:2]) / D + norm_eps)

    def column(h):
        at = slice(h * HD, (h + 1) * HD)
        return (
            p0[:, at].astype(F32) + p1[:, at].astype(F32)
            + p2[:, at].astype(F32) + p3[:, at].astype(F32)
        ) * scale

    def turned(x):
        return x * cosine[...] + pltpu.roll(x, HD // 2, 1) * sine[...]

    factor = math.log2(math.e) / math.sqrt(HD)
    for n in range(heads):
        q = (turned(column(n)) * factor).astype(BF)
        for h in range(HALVES):
            start = (h * heads + n) * span
            queries[start : start + span] = q[h * span : (h + 1) * span]
    near_key[...] = turned(column(heads)).astype(BF)
    near_value[...] = column(heads + 1).astype(BF)
    for copy in copies:
        copy.wait()


def rotate(place, parts, cosine, sine, cache_key, cache_value, before):
    answer = parts[0].shape[0]
    heads = parts[0].shape[1] // HD - 3
    vmem = pl.BlockSpec(memory_space=pltpu.VMEM)
    anywhere = pl.BlockSpec(memory_space=pl.ANY)
    return pl.pallas_call(
        rotate_kernel,
        in_specs=[pl.BlockSpec(memory_space=pltpu.SMEM)] + [vmem] * 6 + [anywhere] * 4,
        out_specs=[vmem] * 3 + [anywhere],
        out_shape=[
            jax.ShapeDtypeStruct((heads * answer, HD), BF),
            jax.ShapeDtypeStruct((answer, HD), BF),
            jax.ShapeDtypeStruct((answer, HD), BF),
            jax.ShapeDtypeStruct((2, cache_key.shape[0] // 2, HD), BF),
        ],
        scratch_shapes=[pltpu.SemaphoreType.DMA((2,))],
        compiler_params=pltpu.CompilerParams(vmem_limit_bytes=16 * MIB),
        cost_estimate=pl.CostEstimate(
            flops=20 * answer * heads * HD, bytes_accessed=3 * MIB, transcendentals=0
        ),
        name="rotate",
    )(place, *parts, cosine, sine, cache_key, cache_value, *before)


def ones_column(rows):
    return jnp.where(lax.broadcasted_iota(jnp.int32, (rows, HD), 1) == 0, 1.0, 0.0).astype(BF)


def fill_section(mask, section, source, slot, local, keys, values):
    ones = ones_column(BLOCK)
    blocks = local // BLOCK

    def fill(b, carry):
        at = pl.ds(pl.multiple_of(slot * local + b * BLOCK, BLOCK), BLOCK)
        bias = jnp.where(mask[section, source * blocks + b] > 0, 0.0, masked_score)
        keys[at, HD:] = jnp.full((BLOCK, HD), bias, F32).astype(BF)
        values[at, HD:] = ones
        return carry

    lax.fori_loop(0, blocks, fill, 0, unroll=4)


def sweep(q_aug, keys, values, buffers, m, acc):
    tile = buffers[0].shape[1]
    tiles = keys.shape[0] // tile
    dims = (((1,), (1,)), ((), ()))

    def score(t):
        s = lax.dot_general(
            q_aug, keys[t * tile : (t + 1) * tile], dims, preferred_element_type=F32
        )
        buffers[t % 2][...] = s
        return jnp.max(s, axis=-1, keepdims=True)

    top = score(0)
    for t in range(tiles):
        m_new = jnp.maximum(m, top)
        if t + 1 < tiles:
            top = score(t + 1)
        p = jnp.exp2(buffers[t % 2][...] - m_new).astype(BF)
        acc = acc * jnp.exp2(m - m_new) + jnp.dot(
            p, values[t * tile : (t + 1) * tile], preferred_element_type=F32
        )
        m = m_new
    return m, acc


def near_kernel(place, mask, queries, near_key, near_value, own_key, own_value, a1, b1, a3, b3,
                out, keys, values, near_values, buf0, buf1, sem):
    section, core = place[0], place[1]
    answer = near_key.shape[0]
    span = answer // HALVES
    rows = queries.shape[0] // HALVES
    local = own_key.shape[0]
    size = local // 2
    sections = mask.shape[1] * BLOCK // local

    copies = []

    def bring(source, buffer, start, size):
        copy = pltpu.make_async_copy(
            source,
            buffer.at[pl.ds(pl.multiple_of(start, size), size), pl.ds(0, HD)],
            sem.at[len(copies)],
        )
        copy.start()
        copies.append(copy)

    bring(own_key, keys, 0, local)
    bring(own_value, values, 0, local)
    for slot, pieces in ((1, (a1, b1)), (2, (a3, b3))):
        for piece, side in zip(pieces, (core, 1 - core)):
            for kind, buffer in ((0, keys), (1, values)):
                bring(piece.at[kind], buffer, slot * local + side * size, size)
    for slot, source in enumerate((section, section + sections - 1, section + 1)):
        fill_section(mask, section, lax.rem(source, sections), slot, local, keys, values)
    near_values[:, :HD] = near_value[...]
    near_values[:, HD:] = ones_column(answer)
    for copy in copies:
        copy.wait()

    ones = ones_column(rows)
    dims = (((1,), (1,)), ((), ()))
    row = lax.rem(lax.broadcasted_iota(jnp.int32, (rows, answer), 0), span)
    column = lax.broadcasted_iota(jnp.int32, (rows, answer), 1)
    lane = lax.broadcasted_iota(jnp.int32, (rows, HD), 1)

    def half(h, carry):
        at = pl.ds(pl.multiple_of(h * rows, rows), rows)
        q = queries[at]
        s = lax.dot_general(q, near_key[...], dims, preferred_element_type=F32)
        s = jnp.where(row + h * span >= column, s, masked_score)
        m = jnp.max(s, axis=-1, keepdims=True)
        acc = jnp.dot(jnp.exp2(s - m).astype(BF), near_values[...], preferred_element_type=F32)
        m, acc = sweep(jnp.concatenate([q, ones], axis=1), keys, values, (buf0, buf1), m, acc)
        out[at, :HD] = acc[:, :HD]
        out[at, HD:] = jnp.where(lane == 1, m, acc[:, HD:])
        return carry

    lax.fori_loop(0, HALVES, half, 0)


def attend_near(place, mask, queries, near_key, near_value, own_key, own_value, pieces):
    rows = queries.shape[0]
    answer = near_key.shape[0]
    context = 3 * own_key.shape[0]
    vmem = pl.BlockSpec(memory_space=pltpu.VMEM)
    smem = pl.BlockSpec(memory_space=pltpu.SMEM)
    anywhere = pl.BlockSpec(memory_space=pl.ANY)
    return pl.pallas_call(
        near_kernel,
        in_specs=[smem, smem] + [vmem] * 3 + [anywhere] * 6,
        out_specs=vmem,
        out_shape=jax.ShapeDtypeStruct((rows, 2 * HD), F32),
        scratch_shapes=[
            pltpu.VMEM((context, 2 * HD), BF),
            pltpu.VMEM((context, 2 * HD), BF),
            pltpu.VMEM((answer, 2 * HD), BF),
            pltpu.VMEM((rows // HALVES, TILE), F32),
            pltpu.VMEM((rows // HALVES, TILE), F32),
            pltpu.SemaphoreType.DMA((10,)),
        ],
        compiler_params=pltpu.CompilerParams(vmem_limit_bytes=32 * MIB),
        cost_estimate=pl.CostEstimate(
            flops=8 * rows * context * HD,
            bytes_accessed=6 * MIB,
            transcendentals=rows * context,
        ),
        name="attend_near",
    )(place, mask, queries, near_key, near_value, own_key, own_value, *pieces)


def far_kernel(place, mask, queries, state, a2, b2, out, keys, values, buf0, buf1, sem):
    section, core = place[0], place[1]
    size = a2.shape[1]
    sections = mask.shape[1] * BLOCK // (2 * size)
    copies = []
    for piece, side in ((a2, core), (b2, 1 - core)):
        for kind, buffer in ((0, keys), (1, values)):
            at = pl.ds(pl.multiple_of(side * size, size), size)
            copies.append(
                pltpu.make_async_copy(
                    piece.at[kind], buffer.at[at, pl.ds(0, HD)], sem.at[len(copies)]
                )
            )
            copies[-1].start()
    source = lax.rem(section + sections - 2, sections)
    fill_section(mask, section, source, 0, 2 * size, keys, values)
    for copy in copies:
        copy.wait()
    rows = queries.shape[0]
    span = out.shape[0]
    q_aug = jnp.concatenate([queries[...], ones_column(rows)], axis=1)
    _, acc = sweep(
        q_aug, keys, values, (buf0, buf1), state[:, HD + 1 : HD + 2], state[...]
    )
    result = (acc[:, :HD] / acc[:, HD : HD + 1]).astype(BF)
    for h in range(rows // span):
        out[:, h * HD : (h + 1) * HD] = result[h * span : (h + 1) * span]


def attend_far(half, place, mask, queries, state, pieces):
    rows = queries.shape[0] // HALVES
    context = 2 * pieces[0].shape[1]
    smem = pl.BlockSpec(memory_space=pltpu.SMEM)
    anywhere = pl.BlockSpec(memory_space=pl.ANY)
    span = ANSWER // HALVES
    return pl.pallas_call(
        far_kernel,
        grid=(1,),
        in_specs=[
            smem,
            smem,
            pl.BlockSpec((rows, HD), lambda i: (half, 0)),
            pl.BlockSpec((rows, 2 * HD), lambda i: (half, 0)),
            anywhere,
            anywhere,
        ],
        out_specs=pl.BlockSpec((span, rows // span * HD), lambda i: (0, 0)),
        out_shape=jax.ShapeDtypeStruct((span, rows // span * HD), BF),
        scratch_shapes=[
            pltpu.VMEM((context, 2 * HD), BF),
            pltpu.VMEM((context, 2 * HD), BF),
            pltpu.VMEM((rows, TILE), F32),
            pltpu.VMEM((rows, TILE), F32),
            pltpu.SemaphoreType.DMA((4,)),
        ],
        compiler_params=pltpu.CompilerParams(vmem_limit_bytes=24 * MIB),
        cost_estimate=pl.CostEstimate(
            flops=8 * rows * context * HD,
            bytes_accessed=3 * MIB,
            transcendentals=rows * context,
        ),
        name="attend_far",
    )(place, mask, queries, state, *pieces)


def output_kernel(place, a0, a1, a2, a3, w_out, before, o0, o1, o2, o3, after, rows, weights, sem):
    count, span, depth = rows.shape
    outs = (o0, o1, o2, o3)
    after[...] = jnp.zeros_like(after)
    width = w_out.shape[1] // len(outs)
    copies = []
    for k in range(len(outs)):
        at = pl.ds(pl.multiple_of(lax.rem(place[2] + k, len(outs)) * width, width), width)
        copies.append(pltpu.make_async_copy(w_out.at[:, at], weights.at[k], sem.at[k]))
        copies[-1].start()
    for r, part in enumerate((a0, a1, a2, a3)):
        rows[lax.rem(place[0] + count - r, count)] = part[...]
    left = rows[...].reshape(count * span, depth)
    for k, out in enumerate(outs):
        copies[k].wait()
        for side in range(2):
            at = slice(side * width // 2, (side + 1) * width // 2)
            out[side] = jnp.dot(left, weights[k, :, at], preferred_element_type=F32).astype(
                out.dtype
            )


def project_out(place, parts, w_out, before):
    span, depth = parts[0].shape
    count = len(parts)
    width = w_out.shape[1] // 4
    vmem = pl.BlockSpec(memory_space=pltpu.VMEM)
    smem = pl.BlockSpec(memory_space=pltpu.SMEM)
    shape = (2, count * span, width // 2)
    return pl.pallas_call(
        output_kernel,
        in_specs=[smem] + [vmem] * count + [pl.BlockSpec(memory_space=pl.ANY)] * 2,
        out_specs=[vmem] * 5,
        out_shape=[jax.ShapeDtypeStruct(shape, F32)]
        + [jax.ShapeDtypeStruct(shape, BF)] * 3
        + [jax.ShapeDtypeStruct((8, 128), F32)],
        scratch_shapes=[
            pltpu.VMEM((count, span, depth), BF),
            pltpu.VMEM((4, depth, width), BF),
            pltpu.SemaphoreType.DMA((4,)),
        ],
        compiler_params=pltpu.CompilerParams(vmem_limit_bytes=24 * MIB),
        cost_estimate=pl.CostEstimate(
            flops=8 * count * span * depth * width, bytes_accessed=6 * MIB, transcendentals=0
        ),
        name="project_out",
    )(place, *parts, w_out, before)


def reduce_kernel(half, place, *refs):
    earlier, pieces, (send, keep) = refs[: 2 * half], refs[2 * half : -2], refs[-2:]
    count, rows, _ = keep.shape
    span = rows // (half + 1)
    for done, out in zip(earlier, (send, keep)):
        out[:, : half * span] = done[...]
    for side, out in ((1 - place[3], send), (place[3], keep)):
        total = pieces[0][side].astype(F32)
        for piece in pieces[1:]:
            total = total + piece[side].astype(F32)
        for c in range(count):
            out[c, half * span :] = total[c * span : (c + 1) * span].astype(out.dtype)


def reduce_pieces(half, place, earlier, pieces, count):
    _, rows, width = pieces[0].shape
    shape = (count, rows // count * (half + 1), width)
    vmem = pl.BlockSpec(memory_space=pltpu.VMEM)
    return pl.pallas_call(
        functools.partial(reduce_kernel, half),
        in_specs=[pl.BlockSpec(memory_space=pltpu.SMEM)] + [vmem] * len((*earlier, *pieces)),
        out_specs=[vmem] * 2,
        out_shape=[jax.ShapeDtypeStruct(shape, BF), jax.ShapeDtypeStruct(shape, F32)],
        compiler_params=pltpu.CompilerParams(vmem_limit_bytes=16 * MIB),
        cost_estimate=pl.CostEstimate(
            flops=8 * rows * width, bytes_accessed=16 * rows * width, transcendentals=0
        ),
        name="reduce_pieces",
    )(place, *earlier, *pieces)


def rotation(answer):
    half = HD // 2
    positions = (NBLK * BLOCK + jnp.arange(answer)).astype(F32)
    frequency = rope_base ** (-2.0 * jnp.arange(half).astype(F32) / HD)
    angles = positions[:, None] * frequency[None, :]
    cosine, sine = jnp.cos(angles), jnp.sin(angles)
    return jnp.concatenate([cosine, cosine], axis=1), jnp.concatenate([-sine, sine], axis=1)


def per_device(
    hidden, norm_gain, w_query, w_key, w_value, w_out, cache_key, cache_value, block_mask
):
    section = lax.axis_index("section")
    core = lax.rem(lax.axis_index("coal"), 2)
    tensor = lax.axis_index("tensor")
    z_hi = lax.rem(tensor, 2)
    place = jnp.stack([section, core, tensor // 2, z_hi]).astype(jnp.int32)
    answer = hidden.shape[1]
    half_rows = cache_key.shape[0] // 2
    piece = jnp.stack(
        [
            lax.dynamic_slice_in_dim(cache_key, core * half_rows, half_rows, 0),
            lax.dynamic_slice_in_dim(cache_value, core * half_rows, half_rows, 0),
        ]
    )
    with jax.named_scope("cache"):
        mine = {r: section_shift(piece, r) for r in (1, 3)}
    with jax.named_scope("swap"):
        other = {r: core_swap(mine[r]) for r in (1, 3)}
    cosine, sine = rotation(answer)

    chunks = project(place, hidden, norm_gain[None, :], w_query, w_key, w_value)
    with jax.named_scope("sums"):
        parts = [chunks[0]] + [section_shift(chunks[r], r) for r in (1, 3, 2)]
    queries, near_key, near_value, piece = rotate(
        place, parts, cosine, sine, cache_key, cache_value, (other[1], other[3])
    )
    with jax.named_scope("cache2"):
        mine[2] = section_shift(piece, 2)
    state = attend_near(
        place, block_mask, queries, near_key, near_value, cache_key, cache_value,
        (mine[1], other[1], mine[3], other[3]),
    )
    with jax.named_scope("swap2"):
        other[2] = core_swap(mine[2] + (state[0, HD + 1] * 0.0).astype(BF))
    attended, gathered = [], []
    for h in range(HALVES):
        attention = attend_far(h, place, block_mask, queries, state, (mine[2], other[2]))
        attended.append(attention)
        with jax.named_scope(f"gather{h}"):
            gathered.append([attention] + [section_shift(attention, r) for r in (1, 2, 3)])

    reduced, turn = (), attended[-1]
    for h in range(HALVES):
        *sums, turn = project_out(place, gathered[h], w_out, turn)
        with jax.named_scope(f"x{h}"):
            pieces = [sums[0]] + [x_shift(sums[r], r) for r in (1, 2, 3)]
        reduced = reduce_pieces(h, place, reduced, pieces, hidden.shape[0])
    send, keep = reduced
    with jax.named_scope("z"):
        arrived = z_swap(send)
    return (keep + arrived.astype(F32)).astype(BF)


def solution(mesh):
    return jax.shard_map(
        per_device,
        mesh=mesh,
        in_specs=(
            P("coal", None, "section"),
            P("section"),
            P("section", "tensor"),
            P("section", "tensor"),
            P("section", "tensor"),
            P("tensor", "section"),
            P("section", "tensor"),
            P("section", "tensor"),
            P("coal", None),
        ),
        out_specs=P("coal", None, ("section", "tensor")),
        check_vma=False,
    )
```

profile of v0, /device:TPU:34, one launch (start us, length us, event | category | flops | bytes accessed | tf_op | source)
XLA Modules:
  0.0 118.5 jit_solution(4527177180679883975)
XLA Ops:
  0.0 1.1 dynamic-slice_bitcast_fusion
  1.1 0.1 pad_maximum_fusion
  1.1 3.1 %collective-permute-start.5 = (bf16[2,1024,128]{2,1,0:T(8,128)(2,1)S(1)}, bf16[2,1024,128]{2,1,0:T(8,128)(2,1)S(1)}, u32[]{:S(2)}, u32[]{:S(2)}) collective-permute-start(bf16[2,1024,128]{2,1,0:T(8,128)(2,1)S(1)} %pad_maximum_fusion), channel_id=1, source_target_pairs={{0,24},{8,0},{16,8},{24,16},{1,25},{9,1},{17,9},{25,17},{2,26},{10... | collective-permute-start | bytes 1572872 | tf_op jit(solution)/shard_map/cache/ppermute | solution.py:28
  4.2 0.0 collective-permute-start.3
  4.2 0.6 pad_add_fusion.place
  4.8 7.5 %project.1 = (bf16[128,1408]{1,0:T(8,128)(2,1)}, bf16[128,1408]{1,0:T(8,128)(2,1)}, bf16[128,1408]{1,0:T(8,128)(2,1)}, bf16[128,1408]{1,0:T(8,128)(2,1)}) custom-call(s32[4]{0:T(128)} %pad_add_fusion.place, bf16[4,128,2048]{2,1,0:T(8,128)(2,1)} %hidden.1, f32[1,2048]{1,0:T(1,128)} %bitcast.10, bf16[2048,1024]{1,0:T(8,128)(2,1)} %w_query.1, ...), custom_call_target="tpu_custom_call" | custom-call | flops 2684354560 | bytes 9437184 | tf_op jit(solution)/shard_map/project/pallas_call | solution.py:103
  12.3 0.0 copy-start.5
  12.3 0.7 collective-permute-start
  13.0 2.7 %collective-permute-start.1 = (bf16[128,1408]{1,0:T(8,128)(2,1)}, bf16[128,1408]{1,0:T(8,128)(2,1)S(1)}, u32[]{:S(2)}, u32[]{:S(2)}) collective-permute-start(bf16[128,1408]{1,0:T(8,128)(2,1)} %get-tuple-element.28), channel_id=1, source_target_pairs={{0,24},{8,0},{16,8},{24,16},{1,25},{9,1},{17,9},{25,17},{2,26},{10... | collective-permute-start | bytes 1081352 | tf_op jit(solution)/shard_map/sums/ppermute | solution.py:28
  15.7 1.4 %collective-permute-start.2 = (bf16[128,1408]{1,0:T(8,128)(2,1)}, bf16[128,1408]{1,0:T(8,128)(2,1)S(1)}, u32[]{:S(2)}, u32[]{:S(2)}) collective-permute-start(bf16[128,1408]{1,0:T(8,128)(2,1)} %get-tuple-element.29), channel_id=1, source_target_pairs={{0,16},{8,24},{16,0},{24,8},{1,17},{9,25},{17,1},{25,9},{2,18},{10... | collective-permute-start | bytes 1081352 | tf_op jit(solution)/shard_map/sums/ppermute | solution.py:28
  17.1 0.0 collective-permute-done.5.a3
  17.1 0.0 collective-permute-start.6
  17.1 3.1 %collective-permute-done.3.a1 = bf16[2,1024,128]{2,1,0:T(8,128)(2,1)S(1)} collective-permute-done((bf16[2,1024,128]{2,1,0:T(8,128)(2,1)S(1)}, bf16[2,1024,128]{2,1,0:T(8,128)(2,1)S(1)}, u32[]{:S(2)}, u32[]{:S(2)}) %collective-permute-start.3) | collective-permute-done | bytes 524320 | tf_op jit(solution)/shard_map/cache/ppermute | solution.py:28
  20.3 0.0 collective-permute-start.4
  20.3 0.3 fusion
  20.6 0.1 pad_maximum_fusion.1
  20.7 13.5 %collective-permute-done.p1 = bf16[128,1408]{1,0:T(8,128)(2,1)S(1)} collective-permute-done((bf16[128,1408]{1,0:T(8,128)(2,1)}, bf16[128,1408]{1,0:T(8,128)(2,1)S(1)}, u32[]{:S(2)}, u32[]{:S(2)}) %collective-permute-start) | collective-permute-done | bytes 360480 | tf_op jit(solution)/shard_map/sums/ppermute | solution.py:28
  34.3 0.0 collective-permute-done.1.p2
  34.3 0.0 collective-permute-done.2.p3
  34.3 0.0 collective-permute-done.6.before3.b3
  34.3 0.0 collective-permute-done.4.before1.b1
  34.3 1.0 copy-done.3
  35.3 1.0 rotate.1
  36.3 0.8 collective-permute-start.7
  37.2 10.4 %attend_near.1.state = f32[1024,256]{1,0:T(8,128)S(1)} custom-call(s32[4]{0:T(128)S(1)} %copy-done.4, s32[4,128]{1,0:T(4,128)S(1)} %copy-done.5, bf16[1024,128]{1,0:T(8,128)(2,1)S(1)} %get-tuple-element.30.queries, bf16[128,128]{1,0:T(8,128)(2,1)S(1)} %get-tuple-element.31.near_key, bf16[128,128]{1,0:T(8,128)(2,1)S(1)} %get-tuple-element.32.near_value, ...), custom_call_target="tpu_custom_call" | custom-call | flops 6442450944 | bytes 6291456 | tf_op jit(solution)/shard_map/attend_near/pallas_call | solution.py:294
  47.6 0.6 slice.4
  48.8 1.1 collective-permute-done.7.a2
  49.9 0.0 copy-start
  49.9 0.1 collective-permute-start.8
  50.0 1.9 %collective-permute-done.8.b2 = bf16[2,1024,128]{2,1,0:T(8,128)(2,1)S(1)} collective-permute-done((bf16[2,1024,128]{2,1,0:T(8,128)(2,1)S(1)}, bf16[2,1024,128]{2,1,0:T(8,128)(2,1)S(1)}, u32[]{:S(2)}, u32[]{:S(2)}) %collective-permute-start.8) | collective-permute-done | bytes 524320 | tf_op jit(solution)/shard_map/swap2/ppermute | solution.py:43
  51.9 3.2 %attend_far.2.a0 = bf16[64,1024]{1,0:T(8,128)(2,1)S(1)} custom-call(s32[4]{0:T(128)S(1)} %copy-done.4, s32[4,128]{1,0:T(4,128)S(1)} %copy-done.5, bf16[1024,128]{1,0:T(8,128)(2,1)S(1)} %get-tuple-element.30.queries, f32[1024,256]{1,0:T(8,128)S(1)} %attend_near.1.state, bf16[2,1024,128]{2,1,0:T(8,128)(2,1)S(1)} %collective-permute-done.7.a2, ...), custom_call_target="tpu_custom_call" | custom-call | flops 1073741824 | bytes 3145728 | tf_op jit(solution)/shard_map/attend_far/pallas_call | solution.py:352
  55.1 0.6 collective-permute-start.11
  55.7 1.5 %collective-permute-start.10 = (bf16[64,1024]{1,0:T(8,128)(2,1)S(1)}, bf16[64,1024]{1,0:T(8,128)(2,1)S(1)}, u32[]{:S(2)}, u32[]{:S(2)}) collective-permute-start(bf16[64,1024]{1,0:T(8,128)(2,1)S(1)} %attend_far.2.a0), channel_id=1, source_target_pairs={{0,16},{8,24},{16,0},{24,8},{1,17},{9,25},{17,1},{25,9},{2,18},{10... | collective-permute-start | bytes 393224 | tf_op jit(solution)/shard_map/gather0/ppermute | solution.py:28
  57.2 1.3 %collective-permute-start.9 = (bf16[64,1024]{1,0:T(8,128)(2,1)S(1)}, bf16[64,1024]{1,0:T(8,128)(2,1)S(1)}, u32[]{:S(2)}, u32[]{:S(2)}) collective-permute-start(bf16[64,1024]{1,0:T(8,128)(2,1)S(1)} %attend_far.2.a0), channel_id=1, source_target_pairs={{0,8},{8,16},{16,24},{24,0},{1,9},{9,17},{17,25},{25,1},{2,10},{10... | collective-permute-start | bytes 393224 | tf_op jit(solution)/shard_map/gather0/ppermute | solution.py:28
  58.5 3.2 %attend_far.3.before.a0 = bf16[64,1024]{1,0:T(8,128)(2,1)S(1)} custom-call(s32[4]{0:T(128)S(1)} %copy-done.4, s32[4,128]{1,0:T(4,128)S(1)} %copy-done.5, bf16[1024,128]{1,0:T(8,128)(2,1)S(1)} %get-tuple-element.30.queries, f32[1024,256]{1,0:T(8,128)S(1)} %attend_near.1.state, bf16[2,1024,128]{2,1,0:T(8,128)(2,1)S(1)} %collective-permute-done.7.a2, ...), custom_call_target="tpu_custom_call" | custom-call | flops 1073741824 | bytes 3145728 | tf_op jit(solution)/shard_map/attend_far/pallas_call | solution.py:352
  61.7 0.0 collective-permute-done.11.a3
  61.7 1.8 %collective-permute-done.10.a2 = bf16[64,1024]{1,0:T(8,128)(2,1)S(1)} collective-permute-done((bf16[64,1024]{1,0:T(8,128)(2,1)S(1)}, bf16[64,1024]{1,0:T(8,128)(2,1)S(1)}, u32[]{:S(2)}, u32[]{:S(2)}) %collective-permute-start.10) | collective-permute-done | bytes 131104 | tf_op jit(solution)/shard_map/gather0/ppermute | solution.py:28
  63.5 1.8 %collective-permute-done.9.a1 = bf16[64,1024]{1,0:T(8,128)(2,1)S(1)} collective-permute-done((bf16[64,1024]{1,0:T(8,128)(2,1)S(1)}, bf16[64,1024]{1,0:T(8,128)(2,1)S(1)}, u32[]{:S(2)}, u32[]{:S(2)}) %collective-permute-start.9) | collective-permute-done | bytes 131104 | tf_op jit(solution)/shard_map/gather0/ppermute | solution.py:28
  65.3 0.0 copy-done
  65.3 3.1 %project_out.2 = (f32[2,256,256]{2,1,0:T(8,128)S(1)}, bf16[2,256,256]{2,1,0:T(8,128)(2,1)S(1)}, bf16[2,256,256]{2,1,0:T(8,128)(2,1)S(1)}, bf16[2,256,256]{2,1,0:T(8,128)(2,1)S(1)}, f32[8,128]{1,0:T(8,128)S(1)}) custom-call(s32[4]{0:T(128)S(1)} %copy-done.4, bf16[64,1024]{1,0:T(8,128)(2,1)S(1)} %attend_far.2.a0, ...), custom_call_target="tpu_custom_call" | custom-call | flops 1073741824 | bytes 6291456 | tf_op jit(solution)/shard_map/project_out/pallas_call | solution.py:411
  68.4 1.6 %collective-permute-start.12 = (bf16[2,256,256]{2,1,0:T(8,128)(2,1)S(1)}, bf16[2,256,256]{2,1,0:T(8,128)(2,1)S(1)}, u32[]{:S(2)}, u32[]{:S(2)}) collective-permute-start(bf16[2,256,256]{2,1,0:T(8,128)(2,1)S(1)} %get-tuple-element.35), channel_id=1, source_target_pairs={{0,2},{1,3},{2,4},{3,5},{4,6},{5,7},{6,0},{7,1},{8,10},{9,11},{10,... | collective-permute-start | bytes 786440 | tf_op jit(solution)/shard_map/x0/ppermute | solution.py:33
  69.9 0.9 collective-permute-start.17
  70.9 1.4 %collective-permute-start.16 = (bf16[64,1024]{1,0:T(8,128)(2,1)S(1)}, bf16[64,1024]{1,0:T(8,128)(2,1)S(1)}, u32[]{:S(2)}, u32[]{:S(2)}) collective-permute-start(bf16[64,1024]{1,0:T(8,128)(2,1)S(1)} %attend_far.3.before.a0), channel_id=1, source_target_pairs={{0,16},{8,24},{16,0},{24,8},{1,17},{9,25},{17,1},{25,9},{2,18},{10... | collective-permute-start | bytes 393224 | tf_op jit(solution)/shard_map/gather1/ppermute | solution.py:28
  72.3 0.8 collective-permute-start.15
  73.1 1.1 collective-permute-start.13
  74.2 2.1 %collective-permute-done.17.a3 = bf16[64,1024]{1,0:T(8,128)(2,1)S(1)} collective-permute-done((bf16[64,1024]{1,0:T(8,128)(2,1)S(1)}, bf16[64,1024]{1,0:T(8,128)(2,1)S(1)}, u32[]{:S(2)}, u32[]{:S(2)}) %collective-permute-start.17) | collective-permute-done | bytes 131104 | tf_op jit(solution)/shard_map/gather1/ppermute | solution.py:28
  76.3 0.5 collective-permute-start.14
  76.9 1.7 %collective-permute-done.16.a2 = bf16[64,1024]{1,0:T(8,128)(2,1)S(1)} collective-permute-done((bf16[64,1024]{1,0:T(8,128)(2,1)S(1)}, bf16[64,1024]{1,0:T(8,128)(2,1)S(1)}, u32[]{:S(2)}, u32[]{:S(2)}) %collective-permute-start.16) | collective-permute-done | bytes 131104 | tf_op jit(solution)/shard_map/gather1/ppermute | solution.py:28
  78.5 0.8 collective-permute-done.15.a1
  79.3 3.2 %project_out.3 = (f32[2,256,256]{2,1,0:T(8,128)S(1)}, bf16[2,256,256]{2,1,0:T(8,128)(2,1)S(1)}, bf16[2,256,256]{2,1,0:T(8,128)(2,1)S(1)}, bf16[2,256,256]{2,1,0:T(8,128)(2,1)S(1)}, f32[8,128]{1,0:T(8,128)}) custom-call(s32[4]{0:T(128)S(1)} %copy-done.4, bf16[64,1024]{1,0:T(8,128)(2,1)S(1)} %attend_far.3.before.a0, ...), custom_call_target="tpu_custom_call" | custom-call | flops 1073741824 | bytes 6291456 | tf_op jit(solution)/shard_map/project_out/pallas_call | solution.py:411
  82.6 1.3 %collective-permute-start.18 = (bf16[2,256,256]{2,1,0:T(8,128)(2,1)S(1)}, bf16[2,256,256]{2,1,0:T(8,128)(2,1)S(1)}, u32[]{:S(2)}, u32[]{:S(2)}) collective-permute-start(bf16[2,256,256]{2,1,0:T(8,128)(2,1)S(1)} %get-tuple-element.42), channel_id=1, source_target_pairs={{0,2},{1,3},{2,4},{3,5},{4,6},{5,7},{6,0},{7,1},{8,10},{9,11},{10,... | collective-permute-start | bytes 786440 | tf_op jit(solution)/shard_map/x1/ppermute | solution.py:33
  83.8 1.4 %collective-permute-start.19 = (bf16[2,256,256]{2,1,0:T(8,128)(2,1)S(1)}, bf16[2,256,256]{2,1,0:T(8,128)(2,1)S(1)}, u32[]{:S(2)}, u32[]{:S(2)}) collective-permute-start(bf16[2,256,256]{2,1,0:T(8,128)(2,1)S(1)} %get-tuple-element.43), channel_id=1, source_target_pairs={{0,4},{1,5},{2,6},{3,7},{4,0},{5,1},{6,2},{7,3},{8,12},{9,13},{10,... | collective-permute-start | bytes 786440 | tf_op jit(solution)/shard_map/x1/ppermute | solution.py:33
  85.2 0.0 collective-permute-done.12.refs_1_
  85.2 1.1 collective-permute-start.20
  86.4 0.0 collective-permute-done.13.refs_2_
  86.4 5.0 %collective-permute-done.14.refs_3_ = bf16[2,256,256]{2,1,0:T(8,128)(2,1)S(1)} collective-permute-done((bf16[2,256,256]{2,1,0:T(8,128)(2,1)S(1)}, bf16[2,256,256]{2,1,0:T(8,128)(2,1)S(1)}, u32[]{:S(2)}, u32[]{:S(2)}) %collective-permute-start.14) | collective-permute-done | bytes 262176 | tf_op jit(solution)/shard_map/x0/ppermute | solution.py:33
  91.4 0.7 reduce_pieces.2
  92.1 0.0 collective-permute-done.18.refs_3_
  92.1 2.7 %collective-permute-done.19.refs_4_ = bf16[2,256,256]{2,1,0:T(8,128)(2,1)S(1)} collective-permute-done((bf16[2,256,256]{2,1,0:T(8,128)(2,1)S(1)}, bf16[2,256,256]{2,1,0:T(8,128)(2,1)S(1)}, u32[]{:S(2)}, u32[]{:S(2)}) %collective-permute-start.19) | collective-permute-done | bytes 262176 | tf_op jit(solution)/shard_map/x1/ppermute | solution.py:33
  94.8 3.8 %collective-permute-done.20.refs_5_ = bf16[2,256,256]{2,1,0:T(8,128)(2,1)S(1)} collective-permute-done((bf16[2,256,256]{2,1,0:T(8,128)(2,1)S(1)}, bf16[2,256,256]{2,1,0:T(8,128)(2,1)S(1)}, u32[]{:S(2)}, u32[]{:S(2)}) %collective-permute-start.20) | collective-permute-done | bytes 262176 | tf_op jit(solution)/shard_map/x1/ppermute | solution.py:33
  98.6 0.7 reduce_pieces.3
  99.3 6.4 %collective-permute-start.21 = (bf16[4,128,256]{2,1,0:T(8,128)(2,1)S(1)}, bf16[4,128,256]{2,1,0:T(8,128)(2,1)S(1)}, u32[]{:S(2)}, u32[]{:S(2)}) collective-permute-start(bf16[4,128,256]{2,1,0:T(8,128)(2,1)S(1)} %get-tuple-element.46), channel_id=1, source_target_pairs={{0,1},{1,0},{2,3},{3,2},{4,5},{5,4},{6,7},{7,6},{8,9},{9,8},{10,11... | collective-permute-start | bytes 786440 | tf_op jit(solution)/shard_map/z/ppermute | solution.py:39
  105.6 12.1 %collective-permute-done.21 = bf16[4,128,256]{2,1,0:T(8,128)(2,1)S(1)} collective-permute-done((bf16[4,128,256]{2,1,0:T(8,128)(2,1)S(1)}, bf16[4,128,256]{2,1,0:T(8,128)(2,1)S(1)}, u32[]{:S(2)}, u32[]{:S(2)}) %collective-permute-start.21) | collective-permute-done | bytes 262176 | tf_op jit(solution)/shard_map/z/ppermute | solution.py:39
  117.8 0.8 add_convert_fusion
  (11 shorter events, 0.1 us)
Async XLA Ops:
  1.1 16.0 %collective-permute-start.5 = (bf16[2,1024,128]{2,1,0:T(8,128)(2,1)S(1)}, bf16[2,1024,128]{2,1,0:T(8,128)(2,1)S(1)}, u32[]{:S(2)}, u32[]{:S(2)}) collective-permute-start(bf16[2,1024,128]{2,1,0:T(8,128)(2,1)S(1)} %pad_maximum_fusion), channel_id=1, source_target_pairs={{0,24},{8,0},{16,8},{24,16},{1,25},{9,1},{17,9},{25,17},{2,26},{10... | collective-permute-start | bytes 1572872 | tf_op jit(solution)/shard_map/cache/ppermute | solution.py:28
  4.2 16.1 %collective-permute-start.3 = (bf16[2,1024,128]{2,1,0:T(8,128)(2,1)S(1)}, bf16[2,1024,128]{2,1,0:T(8,128)(2,1)S(1)}, u32[]{:S(2)}, u32[]{:S(2)}) collective-permute-start(bf16[2,1024,128]{2,1,0:T(8,128)(2,1)S(1)} %pad_maximum_fusion), channel_id=1, source_target_pairs={{0,8},{8,16},{16,24},{24,0},{1,9},{9,17},{17,25},{25,1},{2,10},{10... | collective-permute-start | bytes 1572872 | tf_op jit(solution)/shard_map/cache/ppermute | solution.py:28
  4.8 29.5 %copy-start.1 = (bf16[2048,128]{1,0:T(8,128)(2,1)S(1)}, bf16[2048,128]{1,0:T(8,128)(2,1)}, u32[]{:S(2)}) copy-start(bf16[2048,128]{1,0:T(8,128)(2,1)} %own_key.1) | copy-start | bytes 1572868
  4.8 29.5 %copy-start.2 = (bf16[2048,128]{1,0:T(8,128)(2,1)S(1)}, bf16[2048,128]{1,0:T(8,128)(2,1)}, u32[]{:S(2)}) copy-start(bf16[2048,128]{1,0:T(8,128)(2,1)} %own_value.1) | copy-start | bytes 1572868
  4.8 29.5 %copy-start.4 = (s32[4]{0:T(128)S(1)}, s32[4]{0:T(128)}, u32[]{:S(2)}) copy-start(s32[4]{0:T(128)} %pad_add_fusion.place) | copy-start | bytes 52
  12.3 24.8 %copy-start.5 = (s32[4,128]{1,0:T(4,128)S(1)}, s32[4,128]{1,0:T(4,128)}, u32[]{:S(2)}) copy-start(s32[4,128]{1,0:T(4,128)} %mask.5) | copy-start | bytes 6148
  12.3 21.9 %collective-permute-start = (bf16[128,1408]{1,0:T(8,128)(2,1)}, bf16[128,1408]{1,0:T(8,128)(2,1)S(1)}, u32[]{:S(2)}, u32[]{:S(2)}) collective-permute-start(bf16[128,1408]{1,0:T(8,128)(2,1)} %get-tuple-element.27), channel_id=1, source_target_pairs={{0,8},{8,16},{16,24},{24,0},{1,9},{9,17},{17,25},{25,1},{2,10},{10... | collective-permute-start | bytes 1081352 | tf_op jit(solution)/shard_map/sums/ppermute | solution.py:28
  13.0 21.3 %collective-permute-start.1 = (bf16[128,1408]{1,0:T(8,128)(2,1)}, bf16[128,1408]{1,0:T(8,128)(2,1)S(1)}, u32[]{:S(2)}, u32[]{:S(2)}) collective-permute-start(bf16[128,1408]{1,0:T(8,128)(2,1)} %get-tuple-element.28), channel_id=1, source_target_pairs={{0,24},{8,0},{16,8},{24,16},{1,25},{9,1},{17,9},{25,17},{2,26},{10... | collective-permute-start | bytes 1081352 | tf_op jit(solution)/shard_map/sums/ppermute | solution.py:28
  15.7 18.5 %collective-permute-start.2 = (bf16[128,1408]{1,0:T(8,128)(2,1)}, bf16[128,1408]{1,0:T(8,128)(2,1)S(1)}, u32[]{:S(2)}, u32[]{:S(2)}) collective-permute-start(bf16[128,1408]{1,0:T(8,128)(2,1)} %get-tuple-element.29), channel_id=1, source_target_pairs={{0,16},{8,24},{16,0},{24,8},{1,17},{9,25},{17,1},{25,9},{2,18},{10... | collective-permute-start | bytes 1081352 | tf_op jit(solution)/shard_map/sums/ppermute | solution.py:28
  17.1 17.1 %collective-permute-start.6 = (bf16[2,1024,128]{2,1,0:T(8,128)(2,1)S(1)}, bf16[2,1024,128]{2,1,0:T(8,128)(2,1)S(1)}, u32[]{:S(2)}, u32[]{:S(2)}) collective-permute-start(bf16[2,1024,128]{2,1,0:T(8,128)(2,1)S(1)} %collective-permute-done.5.a3), channel_id=1, source_target_pairs={{0,32},{32,0},{64,96},{96,64},{128,160},{160,128},{192,224},{224,1... | collective-permute-start | bytes 1572872 | tf_op jit(solution)/shard_map/swap/ppermute | solution.py:43
  20.3 14.0 %collective-permute-start.4 = (bf16[2,1024,128]{2,1,0:T(8,128)(2,1)S(1)}, bf16[2,1024,128]{2,1,0:T(8,128)(2,1)S(1)}, u32[]{:S(2)}, u32[]{:S(2)}) collective-permute-start(bf16[2,1024,128]{2,1,0:T(8,128)(2,1)S(1)} %collective-permute-done.3.a1), channel_id=1, source_target_pairs={{0,32},{32,0},{64,96},{96,64},{128,160},{160,128},{192,224},{224,1... | collective-permute-start | bytes 1572872 | tf_op jit(solution)/shard_map/swap/ppermute | solution.py:43
  34.3 1.0 copy-start.3
  36.3 13.6 %collective-permute-start.7 = (bf16[2,1024,128]{2,1,0:T(8,128)(2,1)S(1)}, bf16[2,1024,128]{2,1,0:T(8,128)(2,1)S(1)}, u32[]{:S(2)}, u32[]{:S(2)}) collective-permute-start(bf16[2,1024,128]{2,1,0:T(8,128)(2,1)S(1)} %get-tuple-element.33), channel_id=1, source_target_pairs={{0,16},{8,24},{16,0},{24,8},{1,17},{9,25},{17,1},{25,9},{2,18},{10... | collective-permute-start | bytes 1572872 | tf_op jit(solution)/shard_map/cache2/ppermute | solution.py:28
  49.9 15.4 %copy-start = (bf16[1024,2048]{1,0:T(8,128)(2,1)S(1)}, bf16[1024,2048]{1,0:T(8,128)(2,1)}, u32[]{:S(2)}) copy-start(bf16[1024,2048]{1,0:T(8,128)(2,1)} %w_out.3) | copy-start | bytes 12582916
  49.9 2.0 %collective-permute-start.8 = (bf16[2,1024,128]{2,1,0:T(8,128)(2,1)S(1)}, bf16[2,1024,128]{2,1,0:T(8,128)(2,1)S(1)}, u32[]{:S(2)}, u32[]{:S(2)}) collective-permute-start(bf16[2,1024,128]{2,1,0:T(8,128)(2,1)S(1)} %broadcast_add_fusion), channel_id=1, source_target_pairs={{0,32},{32,0},{64,96},{96,64},{128,160},{160,128},{192,224},{224,1... | collective-permute-start | bytes 1572872 | tf_op jit(solution)/shard_map/swap2/ppermute | solution.py:43
  55.1 6.6 %collective-permute-start.11 = (bf16[64,1024]{1,0:T(8,128)(2,1)S(1)}, bf16[64,1024]{1,0:T(8,128)(2,1)S(1)}, u32[]{:S(2)}, u32[]{:S(2)}) collective-permute-start(bf16[64,1024]{1,0:T(8,128)(2,1)S(1)} %attend_far.2.a0), channel_id=1, source_target_pairs={{0,24},{8,0},{16,8},{24,16},{1,25},{9,1},{17,9},{25,17},{2,26},{10... | collective-permute-start | bytes 393224 | tf_op jit(solution)/shard_map/gather0/ppermute | solution.py:28
  55.7 7.8 %collective-permute-start.10 = (bf16[64,1024]{1,0:T(8,128)(2,1)S(1)}, bf16[64,1024]{1,0:T(8,128)(2,1)S(1)}, u32[]{:S(2)}, u32[]{:S(2)}) collective-permute-start(bf16[64,1024]{1,0:T(8,128)(2,1)S(1)} %attend_far.2.a0), channel_id=1, source_target_pairs={{0,16},{8,24},{16,0},{24,8},{1,17},{9,25},{17,1},{25,9},{2,18},{10... | collective-permute-start | bytes 393224 | tf_op jit(solution)/shard_map/gather0/ppermute | solution.py:28
  57.2 8.1 %collective-permute-start.9 = (bf16[64,1024]{1,0:T(8,128)(2,1)S(1)}, bf16[64,1024]{1,0:T(8,128)(2,1)S(1)}, u32[]{:S(2)}, u32[]{:S(2)}) collective-permute-start(bf16[64,1024]{1,0:T(8,128)(2,1)S(1)} %attend_far.2.a0), channel_id=1, source_target_pairs={{0,8},{8,16},{16,24},{24,0},{1,9},{9,17},{17,25},{25,1},{2,10},{10... | collective-permute-start | bytes 393224 | tf_op jit(solution)/shard_map/gather0/ppermute | solution.py:28
  68.4 16.9 %collective-permute-start.12 = (bf16[2,256,256]{2,1,0:T(8,128)(2,1)S(1)}, bf16[2,256,256]{2,1,0:T(8,128)(2,1)S(1)}, u32[]{:S(2)}, u32[]{:S(2)}) collective-permute-start(bf16[2,256,256]{2,1,0:T(8,128)(2,1)S(1)} %get-tuple-element.35), channel_id=1, source_target_pairs={{0,2},{1,3},{2,4},{3,5},{4,6},{5,7},{6,0},{7,1},{8,10},{9,11},{10,... | collective-permute-start | bytes 786440 | tf_op jit(solution)/shard_map/x0/ppermute | solution.py:33
  69.9 6.4 %collective-permute-start.17 = (bf16[64,1024]{1,0:T(8,128)(2,1)S(1)}, bf16[64,1024]{1,0:T(8,128)(2,1)S(1)}, u32[]{:S(2)}, u32[]{:S(2)}) collective-permute-start(bf16[64,1024]{1,0:T(8,128)(2,1)S(1)} %attend_far.3.before.a0), channel_id=1, source_target_pairs={{0,24},{8,0},{16,8},{24,16},{1,25},{9,1},{17,9},{25,17},{2,26},{10... | collective-permute-start | bytes 393224 | tf_op jit(solution)/shard_map/gather1/ppermute | solution.py:28
  70.9 7.7 %collective-permute-start.16 = (bf16[64,1024]{1,0:T(8,128)(2,1)S(1)}, bf16[64,1024]{1,0:T(8,128)(2,1)S(1)}, u32[]{:S(2)}, u32[]{:S(2)}) collective-permute-start(bf16[64,1024]{1,0:T(8,128)(2,1)S(1)} %attend_far.3.before.a0), channel_id=1, source_target_pairs={{0,16},{8,24},{16,0},{24,8},{1,17},{9,25},{17,1},{25,9},{2,18},{10... | collective-permute-start | bytes 393224 | tf_op jit(solution)/shard_map/gather1/ppermute | solution.py:28
  72.3 7.0 %collective-permute-start.15 = (bf16[64,1024]{1,0:T(8,128)(2,1)S(1)}, bf16[64,1024]{1,0:T(8,128)(2,1)S(1)}, u32[]{:S(2)}, u32[]{:S(2)}) collective-permute-start(bf16[64,1024]{1,0:T(8,128)(2,1)S(1)} %attend_far.3.before.a0), channel_id=1, source_target_pairs={{0,8},{8,16},{16,24},{24,0},{1,9},{9,17},{17,25},{25,1},{2,10},{10... | collective-permute-start | bytes 393224 | tf_op jit(solution)/shard_map/gather1/ppermute | solution.py:28
  73.1 13.3 %collective-permute-start.13 = (bf16[2,256,256]{2,1,0:T(8,128)(2,1)S(1)}, bf16[2,256,256]{2,1,0:T(8,128)(2,1)S(1)}, u32[]{:S(2)}, u32[]{:S(2)}) collective-permute-start(bf16[2,256,256]{2,1,0:T(8,128)(2,1)S(1)} %get-tuple-element.36), channel_id=1, source_target_pairs={{0,4},{1,5},{2,6},{3,7},{4,0},{5,1},{6,2},{7,3},{8,12},{9,13},{10,... | collective-permute-start | bytes 786440 | tf_op jit(solution)/shard_map/x0/ppermute | solution.py:33
  76.3 15.1 %collective-permute-start.14 = (bf16[2,256,256]{2,1,0:T(8,128)(2,1)S(1)}, bf16[2,256,256]{2,1,0:T(8,128)(2,1)S(1)}, u32[]{:S(2)}, u32[]{:S(2)}) collective-permute-start(bf16[2,256,256]{2,1,0:T(8,128)(2,1)S(1)} %get-tuple-element.37), channel_id=1, source_target_pairs={{0,6},{1,7},{2,0},{3,1},{4,2},{5,3},{6,4},{7,5},{8,14},{9,15},{10,... | collective-permute-start | bytes 786440 | tf_op jit(solution)/shard_map/x0/ppermute | solution.py:33
  82.6 9.5 %collective-permute-start.18 = (bf16[2,256,256]{2,1,0:T(8,128)(2,1)S(1)}, bf16[2,256,256]{2,1,0:T(8,128)(2,1)S(1)}, u32[]{:S(2)}, u32[]{:S(2)}) collective-permute-start(bf16[2,256,256]{2,1,0:T(8,128)(2,1)S(1)} %get-tuple-element.42), channel_id=1, source_target_pairs={{0,2},{1,3},{2,4},{3,5},{4,6},{5,7},{6,0},{7,1},{8,10},{9,11},{10,... | collective-permute-start | bytes 786440 | tf_op jit(solution)/shard_map/x1/ppermute | solution.py:33
  83.8 10.9 %collective-permute-start.19 = (bf16[2,256,256]{2,1,0:T(8,128)(2,1)S(1)}, bf16[2,256,256]{2,1,0:T(8,128)(2,1)S(1)}, u32[]{:S(2)}, u32[]{:S(2)}) collective-permute-start(bf16[2,256,256]{2,1,0:T(8,128)(2,1)S(1)} %get-tuple-element.43), channel_id=1, source_target_pairs={{0,4},{1,5},{2,6},{3,7},{4,0},{5,1},{6,2},{7,3},{8,12},{9,13},{10,... | collective-permute-start | bytes 786440 | tf_op jit(solution)/shard_map/x1/ppermute | solution.py:33
  85.2 13.3 %collective-permute-start.20 = (bf16[2,256,256]{2,1,0:T(8,128)(2,1)S(1)}, bf16[2,256,256]{2,1,0:T(8,128)(2,1)S(1)}, u32[]{:S(2)}, u32[]{:S(2)}) collective-permute-start(bf16[2,256,256]{2,1,0:T(8,128)(2,1)S(1)} %get-tuple-element.44), channel_id=1, source_target_pairs={{0,6},{1,7},{2,0},{3,1},{4,2},{5,3},{6,4},{7,5},{8,14},{9,15},{10,... | collective-permute-start | bytes 786440 | tf_op jit(solution)/shard_map/x1/ppermute | solution.py:33
  99.3 18.5 %collective-permute-start.21 = (bf16[4,128,256]{2,1,0:T(8,128)(2,1)S(1)}, bf16[4,128,256]{2,1,0:T(8,128)(2,1)S(1)}, u32[]{:S(2)}, u32[]{:S(2)}) collective-permute-start(bf16[4,128,256]{2,1,0:T(8,128)(2,1)S(1)} %get-tuple-element.46), channel_id=1, source_target_pairs={{0,1},{1,0},{2,3},{3,2},{4,5},{5,4},{6,7},{7,6},{8,9},{9,8},{10,11... | collective-permute-start | bytes 786440 | tf_op jit(solution)/shard_map/z/ppermute | solution.py:39
where the time goes:
time: 119 us
  waiting for transfers between devices  51.5 us (43%)
  Pallas kernels  32.9 us (28%)
  starting transfers between devices  28.8 us (24%)
  local copies, waits for them, and re-layouts  2.65 us (2%)
  other arithmetic  1.84 us (2%)
    ppermute x12, waiting for transfers between devices, section_shift(): return lax.ppermute(x, 'section', [(i, (i + by) % n) for i in range(n)])  26 us
    ppermute x12, starting transfers between devices, section_shift(): return lax.ppermute(x, 'section', [(i, (i + by) % n) for i in range(n)])  15.2 us
    ppermute x1, waiting for transfers between devices, z_swap(): lax.ppermute(x, 'tensor', [(i, i ^ 1) for i in range(lax.axis_size('tenso...  12.1 us
    ppermute x6, waiting for transfers between devices, x_shift(): lax.ppermute(x, 'tensor', [(i, (i // 2 + by) % n * 2 + i % 2) for i in ra...  11.5 us
    pallas_call x1, Pallas kernels, attend_near(): pl.pallas_call(near_kernel, in_specs=[smem, smem] + [vmem] * 3 + [anywher...  10.4 us
    pallas_call x1, Pallas kernels, project(): pl.pallas_call(project_kernel, in_specs=[smem, anywhere, vmem, anywhere,...  7.54 us
    ppermute x6, starting transfers between devices, x_shift(): lax.ppermute(x, 'tensor', [(i, (i // 2 + by) % n * 2 + i % 2) for i in ra...  7.03 us
    ppermute x1, starting transfers between devices, z_swap(): lax.ppermute(x, 'tensor', [(i, i ^ 1) for i in range(lax.axis_size('tenso...  6.37 us
  transfers between devices with their start and end apart: 22, of which 13 were waited for; matrix products, arithmetic and copies ran while one was open for 1% of the time, Pallas kernels for 21%

commit v1 on v0

--- a/solution.py
+++ b/solution.py
@@ -37,6 +37,10 @@
 
 def z_swap(x):
     return lax.ppermute(x, "tensor", [(i, i ^ 1) for i in range(lax.axis_size("tensor"))])
+
+
+def z_neighbour_swap(x):
+    return lax.ppermute(x, "coal", [(i, i ^ 2) for i in range(lax.axis_size("coal"))])
 
 
 def core_swap(x):
@@ -120,8 +124,8 @@
     )(place, hidden, gain, w_query, w_key, w_value)
 
 
-def rotate_kernel(place, p0, p1, p2, p3, cosine, sine, cache_key, cache_value, before1, before3,
-                  queries, near_key, near_value, piece, sem):
+def rotate_kernel(place, p0, p1, p2, p3, cosine, sine, cache_key, cache_value, *rest):
+    queries, near_key, near_value, piece, sem = rest[-5:]
     size = piece.shape[1]
     at = pl.ds(pl.multiple_of(place[1] * size, size), size)
     copies = [
@@ -169,7 +173,8 @@
     anywhere = pl.BlockSpec(memory_space=pl.ANY)
     return pl.pallas_call(
         rotate_kernel,
-        in_specs=[pl.BlockSpec(memory_space=pltpu.SMEM)] + [vmem] * 6 + [anywhere] * 4,
+        in_specs=[pl.BlockSpec(memory_space=pltpu.SMEM)] + [vmem] * 6
+        + [anywhere] * (2 + len(before)),
         out_specs=[vmem] * 3 + [anywhere],
         out_shape=[
             jax.ShapeDtypeStruct((heads * answer, HD), BF),
@@ -229,14 +234,15 @@
     return m, acc
 
 
-def near_kernel(place, mask, queries, near_key, near_value, own_key, own_value, a1, b1, a3, b3,
-                out, keys, values, near_values, buf0, buf1, sem):
-    section, core = place[0], place[1]
+def near_kernel(place, mask, queries, near_key, near_value, own_key, own_value, *rest):
+    quarters, rest = rest[:8], rest[8:]
+    out, keys, values, near_values, buf0, buf1, sem = rest
+    section, quarter = place[0], place[4]
     answer = near_key.shape[0]
     span = answer // HALVES
     rows = queries.shape[0] // HALVES
     local = own_key.shape[0]
-    size = local // 2
+    size = local // 4
     sections = mask.shape[1] * BLOCK // local
 
     copies = []
@@ -252,8 +258,9 @@
 
     bring(own_key, keys, 0, local)
     bring(own_value, values, 0, local)
-    for slot, pieces in ((1, (a1, b1)), (2, (a3, b3))):
-        for piece, side in zip(pieces, (core, 1 - core)):
+    for slot, pieces in ((1, quarters[:4]), (2, quarters[4:])):
+        for n, piece in enumerate(pieces):
+            side = quarter ^ n
             for kind, buffer in ((0, keys), (1, values)):
                 bring(piece.at[kind], buffer, slot * local + side * size, size)
     for slot, source in enumerate((section, section + sections - 1, section + 1)):
@@ -293,7 +300,7 @@
     anywhere = pl.BlockSpec(memory_space=pl.ANY)
     return pl.pallas_call(
         near_kernel,
-        in_specs=[smem, smem] + [vmem] * 3 + [anywhere] * 6,
+        in_specs=[smem, smem] + [vmem] * 3 + [anywhere] * 10,
         out_specs=vmem,
         out_shape=jax.ShapeDtypeStruct((rows, 2 * HD), F32),
         scratch_shapes=[
@@ -302,7 +309,7 @@
             pltpu.VMEM((answer, 2 * HD), BF),
             pltpu.VMEM((rows // HALVES, TILE), F32),
             pltpu.VMEM((rows // HALVES, TILE), F32),
-            pltpu.SemaphoreType.DMA((10,)),
+            pltpu.SemaphoreType.DMA((18,)),
         ],
         compiler_params=pltpu.CompilerParams(vmem_limit_bytes=32 * MIB),
         cost_estimate=pl.CostEstimate(
@@ -428,35 +435,28 @@
     )(place, *parts, w_out, before)
 
 
-def reduce_kernel(half, place, *refs):
-    earlier, pieces, (send, keep) = refs[: 2 * half], refs[2 * half : -2], refs[-2:]
-    count, rows, _ = keep.shape
-    span = rows // (half + 1)
-    for done, out in zip(earlier, (send, keep)):
-        out[:, : half * span] = done[...]
+def reduce_kernel(place, before, *refs):
+    pieces, (send, keep) = refs[:-2], refs[-2:]
     for side, out in ((1 - place[3], send), (place[3], keep)):
         total = pieces[0][side].astype(F32)
         for piece in pieces[1:]:
             total = total + piece[side].astype(F32)
-        for c in range(count):
-            out[c, half * span :] = total[c * span : (c + 1) * span].astype(out.dtype)
-
-
-def reduce_pieces(half, place, earlier, pieces, count):
+        out[...] = total.astype(out.dtype)
+
+
+def reduce_pieces(place, before, pieces):
     _, rows, width = pieces[0].shape
-    shape = (count, rows // count * (half + 1), width)
     vmem = pl.BlockSpec(memory_space=pltpu.VMEM)
     return pl.pallas_call(
-        functools.partial(reduce_kernel, half),
-        in_specs=[pl.BlockSpec(memory_space=pltpu.SMEM)] + [vmem] * len((*earlier, *pieces)),
+        reduce_kernel,
+        in_specs=[pl.BlockSpec(memory_space=pltpu.SMEM), pl.BlockSpec(memory_space=pl.ANY)]
+        + [vmem] * len(pieces),
         out_specs=[vmem] * 2,
-        out_shape=[jax.ShapeDtypeStruct(shape, BF), jax.ShapeDtypeStruct(shape, F32)],
+        out_shape=[jax.ShapeDtypeStruct((rows, width), t) for t in (BF, F32)],
         compiler_params=pltpu.CompilerParams(vmem_limit_bytes=16 * MIB),
-        cost_estimate=pl.CostEstimate(
-            flops=8 * rows * width, bytes_accessed=16 * rows * width, transcendentals=0
-        ),
+        cost_estimate=pl.CostEstimate(flops=8 * rows * width, bytes_accessed=16 * rows * width, transcendentals=0),
         name="reduce_pieces",
-    )(place, *earlier, *pieces)
+    )(place, before, *pieces)
 
 
 def rotation(answer):
@@ -475,52 +475,61 @@
     core = lax.rem(lax.axis_index("coal"), 2)
     tensor = lax.axis_index("tensor")
     z_hi = lax.rem(tensor, 2)
-    place = jnp.stack([section, core, tensor // 2, z_hi]).astype(jnp.int32)
+    quarter = lax.rem(lax.axis_index("coal"), 4)
+    place = jnp.stack([section, core, tensor // 2, z_hi, quarter]).astype(jnp.int32)
     answer = hidden.shape[1]
-    half_rows = cache_key.shape[0] // 2
+    quarter_rows = cache_key.shape[0] // 4
     piece = jnp.stack(
         [
-            lax.dynamic_slice_in_dim(cache_key, core * half_rows, half_rows, 0),
-            lax.dynamic_slice_in_dim(cache_value, core * half_rows, half_rows, 0),
+            lax.dynamic_slice_in_dim(cache_key, quarter * quarter_rows, quarter_rows, 0),
+            lax.dynamic_slice_in_dim(cache_value, quarter * quarter_rows, quarter_rows, 0),
         ]
     )
     with jax.named_scope("cache"):
         mine = {r: section_shift(piece, r) for r in (1, 3)}
-    with jax.named_scope("swap"):
-        other = {r: core_swap(mine[r]) for r in (1, 3)}
+    quarters = []
+    for r in (1, 3):
+        with jax.named_scope("swap"):
+            beside = core_swap(mine[r])
+        with jax.named_scope("zcache"):
+            over = z_neighbour_swap(mine[r])
+        with jax.named_scope("zswap"):
+            both = core_swap(over)
+        quarters += [mine[r], beside, over, both]
     cosine, sine = rotation(answer)
 
     chunks = project(place, hidden, norm_gain[None, :], w_query, w_key, w_value)
     with jax.named_scope("sums"):
         parts = [chunks[0]] + [section_shift(chunks[r], r) for r in (1, 3, 2)]
     queries, near_key, near_value, piece = rotate(
-        place, parts, cosine, sine, cache_key, cache_value, (other[1], other[3])
+        place, parts, cosine, sine, cache_key, cache_value, quarters
     )
     with jax.named_scope("cache2"):
-        mine[2] = section_shift(piece, 2)
+        far_mine = section_shift(piece, 2)
     state = attend_near(
         place, block_mask, queries, near_key, near_value, cache_key, cache_value,
-        (mine[1], other[1], mine[3], other[3]),
+        quarters,
     )
     with jax.named_scope("swap2"):
-        other[2] = core_swap(mine[2] + (state[0, HD + 1] * 0.0).astype(BF))
+        far_other = core_swap(far_mine + (state[0, HD + 1] * 0.0).astype(BF))
     attended, gathered = [], []
     for h in range(HALVES):
-        attention = attend_far(h, place, block_mask, queries, state, (mine[2], other[2]))
+        attention = attend_far(h, place, block_mask, queries, state, (far_mine, far_other))
         attended.append(attention)
         with jax.named_scope(f"gather{h}"):
             gathered.append([attention] + [section_shift(attention, r) for r in (1, 2, 3)])
 
-    reduced, turn = (), attended[-1]
+    turn, send, results = attended[-1], queries, []
     for h in range(HALVES):
         *sums, turn = project_out(place, gathered[h], w_out, turn)
         with jax.named_scope(f"x{h}"):
             pieces = [sums[0]] + [x_shift(sums[r], r) for r in (1, 2, 3)]
-        reduced = reduce_pieces(h, place, reduced, pieces, hidden.shape[0])
-    send, keep = reduced
-    with jax.named_scope("z"):
-        arrived = z_swap(send)
-    return (keep + arrived.astype(F32)).astype(BF)
+        send, keep = reduce_pieces(place, send, pieces)
+        with jax.named_scope(f"z{h}"):
+            arrived = z_swap(send)
+        result = (keep + arrived.astype(F32)).astype(BF)
+        results.append(result.reshape(hidden.shape[0], answer // HALVES, -1))
+    return jnp.concatenate(results, axis=1)
 
 
 def solution(mesh):

time: 119 us -> 115 us (0.966)
  waiting for transfers between devices: 51.5 us -> 37.9 us
  starting transfers between devices: 28.8 us -> 38.6 us
    ppermute x6, waiting for transfers between devices: 11.5 us -> 4.58 us  [x_shift(): lax.ppermute(x, 'tensor', [(i, (i // 2 + by) % n * 2 + i % 2) for i in ra...]
    ppermute x1 -> x2, waiting for transfers between devices: 12.1 us -> 5.71 us  [z_swap(): lax.ppermute(x, 'tensor', [(i, i ^ 1) for i in range(lax.axis_size('tenso...]
    ppermute x1 -> x2, starting transfers between devices: 6.37 us -> 12.4 us  [z_swap(): lax.ppermute(x, 'tensor', [(i, i ^ 1) for i in range(lax.axis_size('tenso...]
    ppermute x0 -> x2, starting transfers between devices: none -> 2.03 us  [z_neighbour_swap(): lax.ppermute(x, 'coal', [(i, i ^ 2) for i in range(lax.axis_size('coal'))])]
    ppermute x3 -> x5, waiting for transfers between devices: 1.9 us -> 2.46 us  [core_swap(): lax.ppermute(x, 'coal', [(i, i ^ 1) for i in range(lax.axis_size('coal'))])]
  transfers between devices with their start and end apart: 22 -> 27, of which waited for: 13 -> 15; matrix products, arithmetic and copies ran while one was open for 1% -> 1% of each run, Pallas kernels for 21% -> 22%
where the time goes in v1:
time: 115 us
  starting transfers between devices  38.6 us (34%)
  waiting for transfers between devices  37.9 us (33%)
  Pallas kernels  33 us (29%)
  local copies, waits for them, and re-layouts  3.18 us (3%)
  other arithmetic  1.26 us (1%)
    ppermute x12, waiting for transfers between devices, section_shift(): return lax.ppermute(x, 'section', [(i, (i + by) % n) for i in range(n)])  25.2 us
    ppermute x12, starting transfers between devices, section_shift(): return lax.ppermute(x, 'section', [(i, (i + by) % n) for i in range(n)])  16.4 us
    ppermute x2, starting transfers between devices, z_swap(): lax.ppermute(x, 'tensor', [(i, i ^ 1) for i in range(lax.axis_size('tenso...  12.4 us
    pallas_call x1, Pallas kernels, attend_near(): pl.pallas_call(near_kernel, in_specs=[smem, smem] + [vmem] * 3 + [anywher...  10.5 us
    pallas_call x1, Pallas kernels, project(): pl.pallas_call(project_kernel, in_specs=[smem, anywhere, vmem, anywhere,...  7.55 us
    ppermute x6, starting transfers between devices, x_shift(): lax.ppermute(x, 'tensor', [(i, (i // 2 + by) % n * 2 + i % 2) for i in ra...  7.05 us
    pallas_call x2, Pallas kernels, attend_far(): pl.pallas_call(far_kernel, grid=(1,), in_specs=[smem, smem, pl.BlockSpec(...  6.31 us
    pallas_call x2, Pallas kernels, project_out(): pl.pallas_call(output_kernel, in_specs=[smem] + [vmem] * count + [pl.Bloc...  6.3 us
  transfers between devices with their start and end apart: 27, of which 15 were waited for; matrix products, arithmetic and copies ran while one was open for 1% of the time, Pallas kernels for 22%

profile of v1, /device:TPU:34, one launch (start us, length us, event | category | flops | bytes accessed | tf_op | source)
XLA Modules:
  0.0 114.7 jit_solution(12897438325172226840)
XLA Ops:
  0.0 1.0 dynamic-slice_bitcast_fusion
  1.0 3.1 %collective-permute-start.7 = (bf16[2,512,128]{2,1,0:T(8,128)(2,1)S(1)}, bf16[2,512,128]{2,1,0:T(8,128)(2,1)S(1)}, u32[]{:S(2)}, u32[]{:S(2)}) collective-permute-start(bf16[2,512,128]{2,1,0:T(8,128)(2,1)S(1)} %pad_maximum_fusion), channel_id=1, source_target_pairs={{0,24},{8,0},{16,8},{24,16},{1,25},{9,1},{17,9},{25,17},{2,26},{10... | collective-permute-start | bytes 786440 | tf_op jit(solution)/shard_map/cache/ppermute | solution.py:28
  4.1 0.0 collective-permute-start.3
  4.1 0.6 stack.32.place
  4.7 7.6 %project.1 = (bf16[128,1408]{1,0:T(8,128)(2,1)}, bf16[128,1408]{1,0:T(8,128)(2,1)}, bf16[128,1408]{1,0:T(8,128)(2,1)}, bf16[128,1408]{1,0:T(8,128)(2,1)}) custom-call(s32[5]{0:T(128)} %stack.32.place, bf16[4,128,2048]{2,1,0:T(8,128)(2,1)} %hidden.1, f32[1,2048]{1,0:T(1,128)} %bitcast.15, bf16[2048,1024]{1,0:T(8,128)(2,1)} %w_query.1, ...), custom_call_target="tpu_custom_call" | custom-call | flops 2684354560 | bytes 9437184 | tf_op jit(solution)/shard_map/project/pallas_call | solution.py:107
  12.3 0.0 copy-start.5
  12.3 0.7 collective-permute-start
  13.0 2.7 %collective-permute-start.1 = (bf16[128,1408]{1,0:T(8,128)(2,1)}, bf16[128,1408]{1,0:T(8,128)(2,1)S(1)}, u32[]{:S(2)}, u32[]{:S(2)}) collective-permute-start(bf16[128,1408]{1,0:T(8,128)(2,1)} %get-tuple-element.28), channel_id=1, source_target_pairs={{0,24},{8,0},{16,8},{24,16},{1,25},{9,1},{17,9},{25,17},{2,26},{10... | collective-permute-start | bytes 1081352 | tf_op jit(solution)/shard_map/sums/ppermute | solution.py:28
  15.7 0.0 collective-permute-done.7.rest_4_
  15.7 0.1 collective-permute-start.9
  15.8 0.0 collective-permute-done.3.rest_0_
  15.8 1.9 %collective-permute-start.5 = (bf16[2,512,128]{2,1,0:T(8,128)(2,1)S(1)}, bf16[2,512,128]{2,1,0:T(8,128)(2,1)S(1)}, u32[]{:S(2)}, u32[]{:S(2)}) collective-permute-start(bf16[2,512,128]{2,1,0:T(8,128)(2,1)S(1)} %collective-permute-done.3.rest_0_), channel_id=1, source_target_pairs={{0,64},{32,96},{64,0},{96,32},{128,192},{160,224},{192,128},{224,1... | collective-permute-start | bytes 786440 | tf_op jit(solution)/shard_map/zcache/ppermute | solution.py:43
  17.7 1.4 %collective-permute-start.2 = (bf16[128,1408]{1,0:T(8,128)(2,1)}, bf16[128,1408]{1,0:T(8,128)(2,1)S(1)}, u32[]{:S(2)}, u32[]{:S(2)}) collective-permute-start(bf16[128,1408]{1,0:T(8,128)(2,1)} %get-tuple-element.29), channel_id=1, source_target_pairs={{0,16},{8,24},{16,0},{24,8},{1,17},{9,25},{17,1},{25,9},{2,18},{10... | collective-permute-start | bytes 1081352 | tf_op jit(solution)/shard_map/sums/ppermute | solution.py:28
  19.1 5.1 %collective-permute-done.p1 = bf16[128,1408]{1,0:T(8,128)(2,1)S(1)} collective-permute-done((bf16[128,1408]{1,0:T(8,128)(2,1)}, bf16[128,1408]{1,0:T(8,128)(2,1)S(1)}, u32[]{:S(2)}, u32[]{:S(2)}) %collective-permute-start) | collective-permute-done | bytes 360480 | tf_op jit(solution)/shard_map/sums/ppermute | solution.py:28
  24.3 0.0 collective-permute-start.8
  24.3 6.6 %collective-permute-done.1.p2 = bf16[128,1408]{1,0:T(8,128)(2,1)S(1)} collective-permute-done((bf16[128,1408]{1,0:T(8,128)(2,1)}, bf16[128,1408]{1,0:T(8,128)(2,1)S(1)}, u32[]{:S(2)}, u32[]{:S(2)}) %collective-permute-start.1) | collective-permute-done | bytes 360480 | tf_op jit(solution)/shard_map/sums/ppermute | solution.py:28
  30.9 0.0 collective-permute-start.4
  30.9 0.0 collective-permute-done.9.rest_6_
  30.9 0.5 collective-permute-start.10
  31.4 0.1 collective-permute-start.6
  31.5 0.3 fusion
  31.8 0.1 pad_maximum_fusion.2
  31.9 0.7 collective-permute-done.2.p3
  32.6 0.2 collective-permute-done.10.rest_7_
  32.8 0.4 collective-permute-done.6.rest_3_
  33.2 1.0 copy-done.3
  34.1 1.0 rotate.1
  35.2 1.9 %collective-permute-start.11 = (bf16[2,1024,128]{2,1,0:T(8,128)(2,1)S(1)}, bf16[2,1024,128]{2,1,0:T(8,128)(2,1)S(1)}, u32[]{:S(2)}, u32[]{:S(2)}) collective-permute-start(bf16[2,1024,128]{2,1,0:T(8,128)(2,1)S(1)} %get-tuple-element.33), channel_id=1, source_target_pairs={{0,16},{8,24},{16,0},{24,8},{1,17},{9,25},{17,1},{25,9},{2,18},{10... | collective-permute-start | bytes 1572872 | tf_op jit(solution)/shard_map/cache2/ppermute | solution.py:28
  37.1 10.5 %attend_near.1.state = f32[1024,256]{1,0:T(8,128)S(1)} custom-call(s32[5]{0:T(128)S(1)} %copy-done.4, s32[4,128]{1,0:T(4,128)S(1)} %copy-done.5, bf16[1024,128]{1,0:T(8,128)(2,1)S(1)} %get-tuple-element.30.queries.before, bf16[128,128]{1,0:T(8,128)(2,1)S(1)} %get-tuple-element.31.near_key, bf16[128,128]{1,0:T(8,128)(2,1)S(1)} %get-tuple-element.32.near_value, ...), custom_call_target="tpu_custom_call" | custom-call | flops 6442450944 | bytes 6291456 | tf_op jit(solution)/shard_map/attend_near/pallas_call | solution.py:301
  47.6 0.6 slice.4
  48.8 2.1 %collective-permute-done.11.a2 = bf16[2,1024,128]{2,1,0:T(8,128)(2,1)S(1)} collective-permute-done((bf16[2,1024,128]{2,1,0:T(8,128)(2,1)S(1)}, bf16[2,1024,128]{2,1,0:T(8,128)(2,1)S(1)}, u32[]{:S(2)}, u32[]{:S(2)}) %collective-permute-start.11) | collective-permute-done | bytes 524320 | tf_op jit(solution)/shard_map/cache2/ppermute | solution.py:28
  51.0 0.0 copy-start
  51.0 0.1 collective-permute-start.12
  51.1 1.9 %collective-permute-done.12.b2 = bf16[2,1024,128]{2,1,0:T(8,128)(2,1)S(1)} collective-permute-done((bf16[2,1024,128]{2,1,0:T(8,128)(2,1)S(1)}, bf16[2,1024,128]{2,1,0:T(8,128)(2,1)S(1)}, u32[]{:S(2)}, u32[]{:S(2)}) %collective-permute-start.12) | collective-permute-done | bytes 524320 | tf_op jit(solution)/shard_map/swap2/ppermute | solution.py:47
  53.0 3.2 %attend_far.2.a0 = bf16[64,1024]{1,0:T(8,128)(2,1)S(1)} custom-call(s32[5]{0:T(128)S(1)} %copy-done.4, s32[4,128]{1,0:T(4,128)S(1)} %copy-done.5, bf16[1024,128]{1,0:T(8,128)(2,1)S(1)} %get-tuple-element.30.queries.before, f32[1024,256]{1,0:T(8,128)S(1)} %attend_near.1.state, bf16[2,1024,128]{2,1,0:T(8,128)(2,1)S(1)} %collective-permute-done.11.a2, ...), custom_call_target="tpu_custom_call" | custom-call | flops 1073741824 | bytes 3145728 | tf_op jit(solution)/shard_map/attend_far/pallas_call | solution.py:359
  56.1 3.7 %collective-permute-start.15 = (bf16[64,1024]{1,0:T(8,128)(2,1)S(1)}, bf16[64,1024]{1,0:T(8,128)(2,1)S(1)}, u32[]{:S(2)}, u32[]{:S(2)}) collective-permute-start(bf16[64,1024]{1,0:T(8,128)(2,1)S(1)} %attend_far.2.a0), channel_id=1, source_target_pairs={{0,24},{8,0},{16,8},{24,16},{1,25},{9,1},{17,9},{25,17},{2,26},{10... | collective-permute-start | bytes 393224 | tf_op jit(solution)/shard_map/gather0/ppermute | solution.py:28
  59.8 0.0 collective-permute-start.14
  59.8 1.0 collective-permute-start.13
  60.7 3.2 %attend_far.3.before.a0 = bf16[64,1024]{1,0:T(8,128)(2,1)S(1)} custom-call(s32[5]{0:T(128)S(1)} %copy-done.4, s32[4,128]{1,0:T(4,128)S(1)} %copy-done.5, bf16[1024,128]{1,0:T(8,128)(2,1)S(1)} %get-tuple-element.30.queries.before, f32[1024,256]{1,0:T(8,128)S(1)} %attend_near.1.state, bf16[2,1024,128]{2,1,0:T(8,128)(2,1)S(1)} %collective-permute-done.11.a2, ...), custom_call_target="tpu_custom_call" | custom-call | flops 1073741824 | bytes 3145728 | tf_op jit(solution)/shard_map/attend_far/pallas_call | solution.py:359
  63.9 1.7 %collective-permute-done.15.a3 = bf16[64,1024]{1,0:T(8,128)(2,1)S(1)} collective-permute-done((bf16[64,1024]{1,0:T(8,128)(2,1)S(1)}, bf16[64,1024]{1,0:T(8,128)(2,1)S(1)}, u32[]{:S(2)}, u32[]{:S(2)}) %collective-permute-start.15) | collective-permute-done | bytes 131104 | tf_op jit(solution)/shard_map/gather0/ppermute | solution.py:28
  65.7 2.0 %collective-permute-done.14.a2 = bf16[64,1024]{1,0:T(8,128)(2,1)S(1)} collective-permute-done((bf16[64,1024]{1,0:T(8,128)(2,1)S(1)}, bf16[64,1024]{1,0:T(8,128)(2,1)S(1)}, u32[]{:S(2)}, u32[]{:S(2)}) %collective-permute-start.14) | collective-permute-done | bytes 131104 | tf_op jit(solution)/shard_map/gather0/ppermute | solution.py:28
  67.7 1.4 %collective-permute-done.13.a1 = bf16[64,1024]{1,0:T(8,128)(2,1)S(1)} collective-permute-done((bf16[64,1024]{1,0:T(8,128)(2,1)S(1)}, bf16[64,1024]{1,0:T(8,128)(2,1)S(1)}, u32[]{:S(2)}, u32[]{:S(2)}) %collective-permute-start.13) | collective-permute-done | bytes 131104 | tf_op jit(solution)/shard_map/gather0/ppermute | solution.py:28
  69.1 3.1 %project_out.2 = (f32[2,256,256]{2,1,0:T(8,128)S(1)}, bf16[2,256,256]{2,1,0:T(8,128)(2,1)S(1)}, bf16[2,256,256]{2,1,0:T(8,128)(2,1)S(1)}, bf16[2,256,256]{2,1,0:T(8,128)(2,1)S(1)}, f32[8,128]{1,0:T(8,128)S(1)}) custom-call(s32[5]{0:T(128)S(1)} %copy-done.4, bf16[64,1024]{1,0:T(8,128)(2,1)S(1)} %attend_far.2.a0, ...), custom_call_target="tpu_custom_call" | custom-call | flops 1073741824 | bytes 6291456 | tf_op jit(solution)/shard_map/project_out/pallas_call | solution.py:418
  72.2 1.6 %collective-permute-start.16 = (bf16[2,256,256]{2,1,0:T(8,128)(2,1)S(1)}, bf16[2,256,256]{2,1,0:T(8,128)(2,1)S(1)}, u32[]{:S(2)}, u32[]{:S(2)}) collective-permute-start(bf16[2,256,256]{2,1,0:T(8,128)(2,1)S(1)} %get-tuple-element.35), channel_id=1, source_target_pairs={{0,2},{1,3},{2,4},{3,5},{4,6},{5,7},{6,0},{7,1},{8,10},{9,11},{10,... | collective-permute-start | bytes 786440 | tf_op jit(solution)/shard_map/x0/ppermute | solution.py:33
  73.7 0.9 collective-permute-start.22
  74.6 0.2 collective-permute-start.21
  74.9 0.9 collective-permute-start.20
  75.8 1.1 collective-permute-start.17
  76.9 3.1 %collective-permute-done.22.a3 = bf16[64,1024]{1,0:T(8,128)(2,1)S(1)} collective-permute-done((bf16[64,1024]{1,0:T(8,128)(2,1)S(1)}, bf16[64,1024]{1,0:T(8,128)(2,1)S(1)}, u32[]{:S(2)}, u32[]{:S(2)}) %collective-permute-start.22) | collective-permute-done | bytes 131104 | tf_op jit(solution)/shard_map/gather1/ppermute | solution.py:28
  80.0 0.5 collective-permute-start.18
  80.5 1.7 %collective-permute-done.21.a2 = bf16[64,1024]{1,0:T(8,128)(2,1)S(1)} collective-permute-done((bf16[64,1024]{1,0:T(8,128)(2,1)S(1)}, bf16[64,1024]{1,0:T(8,128)(2,1)S(1)}, u32[]{:S(2)}, u32[]{:S(2)}) %collective-permute-start.21) | collective-permute-done | bytes 131104 | tf_op jit(solution)/shard_map/gather1/ppermute | solution.py:28
  82.2 0.7 collective-permute-done.20.a1
  82.9 3.2 %project_out.3 = (f32[2,256,256]{2,1,0:T(8,128)S(1)}, bf16[2,256,256]{2,1,0:T(8,128)(2,1)S(1)}, bf16[2,256,256]{2,1,0:T(8,128)(2,1)S(1)}, bf16[2,256,256]{2,1,0:T(8,128)(2,1)S(1)}, f32[8,128]{1,0:T(8,128)}) custom-call(s32[5]{0:T(128)S(1)} %copy-done.4, bf16[64,1024]{1,0:T(8,128)(2,1)S(1)} %attend_far.3.before.a0, ...), custom_call_target="tpu_custom_call" | custom-call | flops 1073741824 | bytes 6291456 | tf_op jit(solution)/shard_map/project_out/pallas_call | solution.py:418
  86.1 1.3 %collective-permute-start.23 = (bf16[2,256,256]{2,1,0:T(8,128)(2,1)S(1)}, bf16[2,256,256]{2,1,0:T(8,128)(2,1)S(1)}, u32[]{:S(2)}, u32[]{:S(2)}) collective-permute-start(bf16[2,256,256]{2,1,0:T(8,128)(2,1)S(1)} %get-tuple-element.42), channel_id=1, source_target_pairs={{0,2},{1,3},{2,4},{3,5},{4,6},{5,7},{6,0},{7,1},{8,10},{9,11},{10,... | collective-permute-start | bytes 786440 | tf_op jit(solution)/shard_map/x1/ppermute | solution.py:33
  87.4 1.4 %collective-permute-start.24 = (bf16[2,256,256]{2,1,0:T(8,128)(2,1)S(1)}, bf16[2,256,256]{2,1,0:T(8,128)(2,1)S(1)}, u32[]{:S(2)}, u32[]{:S(2)}) collective-permute-start(bf16[2,256,256]{2,1,0:T(8,128)(2,1)S(1)} %get-tuple-element.43), channel_id=1, source_target_pairs={{0,4},{1,5},{2,6},{3,7},{4,0},{5,1},{6,2},{7,3},{8,12},{9,13},{10,... | collective-permute-start | bytes 786440 | tf_op jit(solution)/shard_map/x1/ppermute | solution.py:33
  88.8 1.1 collective-permute-start.25
  89.9 0.0 collective-permute-done.17.refs_2_
  89.9 4.6 %collective-permute-done.18.refs_3_ = bf16[2,256,256]{2,1,0:T(8,128)(2,1)S(1)} collective-permute-done((bf16[2,256,256]{2,1,0:T(8,128)(2,1)S(1)}, bf16[2,256,256]{2,1,0:T(8,128)(2,1)S(1)}, u32[]{:S(2)}, u32[]{:S(2)}) %collective-permute-start.18) | collective-permute-done | bytes 262176 | tf_op jit(solution)/shard_map/x0/ppermute | solution.py:33
  94.5 0.7 reduce_pieces.2
  95.2 6.4 %collective-permute-start.19 = (bf16[256,256]{1,0:T(8,128)(2,1)S(1)}, bf16[256,256]{1,0:T(8,128)(2,1)S(1)}, u32[]{:S(2)}, u32[]{:S(2)}) collective-permute-start(bf16[256,256]{1,0:T(8,128)(2,1)S(1)} %get-tuple-element.39.before), channel_id=1, source_target_pairs={{0,1},{1,0},{2,3},{3,2},{4,5},{5,4},{6,7},{7,6},{8,9},{9,8},{10,11... | collective-permute-start | bytes 393224 | tf_op jit(solution)/shard_map/z0/ppermute | solution.py:39
  101.6 0.7 reduce_pieces.3
  102.3 6.0 %collective-permute-start.26 = (bf16[256,256]{1,0:T(8,128)(2,1)S(1)}, bf16[256,256]{1,0:T(8,128)(2,1)S(1)}, u32[]{:S(2)}, u32[]{:S(2)}) collective-permute-start(bf16[256,256]{1,0:T(8,128)(2,1)S(1)} %get-tuple-element.46), channel_id=1, source_target_pairs={{0,1},{1,0},{2,3},{3,2},{4,5},{5,4},{6,7},{7,6},{8,9},{9,8},{10,11... | collective-permute-start | bytes 393224 | tf_op jit(solution)/shard_map/z1/ppermute | solution.py:39
  108.3 5.7 %collective-permute-done.26 = bf16[256,256]{1,0:T(8,128)(2,1)S(1)} collective-permute-done((bf16[256,256]{1,0:T(8,128)(2,1)S(1)}, bf16[256,256]{1,0:T(8,128)(2,1)S(1)}, u32[]{:S(2)}, u32[]{:S(2)}) %collective-permute-start.26) | collective-permute-done | bytes 131104 | tf_op jit(solution)/shard_map/z1/ppermute | solution.py:39
  114.0 0.7 pad_maximum_fusion.1
  (23 shorter events, 0.2 us)
Async XLA Ops:
  1.0 14.7 %collective-permute-start.7 = (bf16[2,512,128]{2,1,0:T(8,128)(2,1)S(1)}, bf16[2,512,128]{2,1,0:T(8,128)(2,1)S(1)}, u32[]{:S(2)}, u32[]{:S(2)}) collective-permute-start(bf16[2,512,128]{2,1,0:T(8,128)(2,1)S(1)} %pad_maximum_fusion), channel_id=1, source_target_pairs={{0,24},{8,0},{16,8},{24,16},{1,25},{9,1},{17,9},{25,17},{2,26},{10... | collective-permute-start | bytes 786440 | tf_op jit(solution)/shard_map/cache/ppermute | solution.py:28
  4.1 11.7 %collective-permute-start.3 = (bf16[2,512,128]{2,1,0:T(8,128)(2,1)S(1)}, bf16[2,512,128]{2,1,0:T(8,128)(2,1)S(1)}, u32[]{:S(2)}, u32[]{:S(2)}) collective-permute-start(bf16[2,512,128]{2,1,0:T(8,128)(2,1)S(1)} %pad_maximum_fusion), channel_id=1, source_target_pairs={{0,8},{8,16},{16,24},{24,0},{1,9},{9,17},{17,25},{25,1},{2,10},{10... | collective-permute-start | bytes 786440 | tf_op jit(solution)/shard_map/cache/ppermute | solution.py:28
  4.7 28.4 %copy-start.1 = (bf16[2048,128]{1,0:T(8,128)(2,1)S(1)}, bf16[2048,128]{1,0:T(8,128)(2,1)}, u32[]{:S(2)}) copy-start(bf16[2048,128]{1,0:T(8,128)(2,1)} %own_key.1) | copy-start | bytes 1572868
  4.7 28.4 %copy-start.2 = (bf16[2048,128]{1,0:T(8,128)(2,1)S(1)}, bf16[2048,128]{1,0:T(8,128)(2,1)}, u32[]{:S(2)}) copy-start(bf16[2048,128]{1,0:T(8,128)(2,1)} %own_value.1) | copy-start | bytes 1572868
  4.7 28.4 %copy-start.4 = (s32[5]{0:T(128)S(1)}, s32[5]{0:T(128)}, u32[]{:S(2)}) copy-start(s32[5]{0:T(128)} %stack.32.place) | copy-start | bytes 64
  12.3 24.8 %copy-start.5 = (s32[4,128]{1,0:T(4,128)S(1)}, s32[4,128]{1,0:T(4,128)}, u32[]{:S(2)}) copy-start(s32[4,128]{1,0:T(4,128)} %mask.5) | copy-start | bytes 6148
  12.3 12.0 %collective-permute-start = (bf16[128,1408]{1,0:T(8,128)(2,1)}, bf16[128,1408]{1,0:T(8,128)(2,1)S(1)}, u32[]{:S(2)}, u32[]{:S(2)}) collective-permute-start(bf16[128,1408]{1,0:T(8,128)(2,1)} %get-tuple-element.27), channel_id=1, source_target_pairs={{0,8},{8,16},{16,24},{24,0},{1,9},{9,17},{17,25},{25,1},{2,10},{10... | collective-permute-start | bytes 1081352 | tf_op jit(solution)/shard_map/sums/ppermute | solution.py:28
  13.0 17.9 %collective-permute-start.1 = (bf16[128,1408]{1,0:T(8,128)(2,1)}, bf16[128,1408]{1,0:T(8,128)(2,1)S(1)}, u32[]{:S(2)}, u32[]{:S(2)}) collective-permute-start(bf16[128,1408]{1,0:T(8,128)(2,1)} %get-tuple-element.28), channel_id=1, source_target_pairs={{0,24},{8,0},{16,8},{24,16},{1,25},{9,1},{17,9},{25,17},{2,26},{10... | collective-permute-start | bytes 1081352 | tf_op jit(solution)/shard_map/sums/ppermute | solution.py:28
  15.7 15.2 %collective-permute-start.9 = (bf16[2,512,128]{2,1,0:T(8,128)(2,1)S(1)}, bf16[2,512,128]{2,1,0:T(8,128)(2,1)S(1)}, u32[]{:S(2)}, u32[]{:S(2)}) collective-permute-start(bf16[2,512,128]{2,1,0:T(8,128)(2,1)S(1)} %collective-permute-done.7.rest_4_), channel_id=1, source_target_pairs={{0,64},{32,96},{64,0},{96,32},{128,192},{160,224},{192,128},{224,1... | collective-permute-start | bytes 786440 | tf_op jit(solution)/shard_map/zcache/ppermute | solution.py:43
  15.8 15.6 %collective-permute-start.5 = (bf16[2,512,128]{2,1,0:T(8,128)(2,1)S(1)}, bf16[2,512,128]{2,1,0:T(8,128)(2,1)S(1)}, u32[]{:S(2)}, u32[]{:S(2)}) collective-permute-start(bf16[2,512,128]{2,1,0:T(8,128)(2,1)S(1)} %collective-permute-done.3.rest_0_), channel_id=1, source_target_pairs={{0,64},{32,96},{64,0},{96,32},{128,192},{160,224},{192,128},{224,1... | collective-permute-start | bytes 786440 | tf_op jit(solution)/shard_map/zcache/ppermute | solution.py:43
  17.7 14.8 %collective-permute-start.2 = (bf16[128,1408]{1,0:T(8,128)(2,1)}, bf16[128,1408]{1,0:T(8,128)(2,1)S(1)}, u32[]{:S(2)}, u32[]{:S(2)}) collective-permute-start(bf16[128,1408]{1,0:T(8,128)(2,1)} %get-tuple-element.29), channel_id=1, source_target_pairs={{0,16},{8,24},{16,0},{24,8},{1,17},{9,25},{17,1},{25,9},{2,18},{10... | collective-permute-start | bytes 1081352 | tf_op jit(solution)/shard_map/sums/ppermute | solution.py:28
  24.3 8.3 %collective-permute-start.8 = (bf16[2,512,128]{2,1,0:T(8,128)(2,1)S(1)}, bf16[2,512,128]{2,1,0:T(8,128)(2,1)S(1)}, u32[]{:S(2)}, u32[]{:S(2)}) collective-permute-start(bf16[2,512,128]{2,1,0:T(8,128)(2,1)S(1)} %collective-permute-done.7.rest_4_), channel_id=1, source_target_pairs={{0,32},{32,0},{64,96},{96,64},{128,160},{160,128},{192,224},{224,1... | collective-permute-start | bytes 786440 | tf_op jit(solution)/shard_map/swap/ppermute | solution.py:47
  30.9 1.7 %collective-permute-start.4 = (bf16[2,512,128]{2,1,0:T(8,128)(2,1)S(1)}, bf16[2,512,128]{2,1,0:T(8,128)(2,1)S(1)}, u32[]{:S(2)}, u32[]{:S(2)}) collective-permute-start(bf16[2,512,128]{2,1,0:T(8,128)(2,1)S(1)} %collective-permute-done.3.rest_0_), channel_id=1, source_target_pairs={{0,32},{32,0},{64,96},{96,64},{128,160},{160,128},{192,224},{224,1... | collective-permute-start | bytes 786440 | tf_op jit(solution)/shard_map/swap/ppermute | solution.py:47
  30.9 1.9 %collective-permute-start.10 = (bf16[2,512,128]{2,1,0:T(8,128)(2,1)S(1)}, bf16[2,512,128]{2,1,0:T(8,128)(2,1)S(1)}, u32[]{:S(2)}, u32[]{:S(2)}) collective-permute-start(bf16[2,512,128]{2,1,0:T(8,128)(2,1)S(1)} %collective-permute-done.9.rest_6_), channel_id=1, source_target_pairs={{0,32},{32,0},{64,96},{96,64},{128,160},{160,128},{192,224},{224,1... | collective-permute-start | bytes 786440 | tf_op jit(solution)/shard_map/zswap/ppermute | solution.py:47
  31.4 1.8 %collective-permute-start.6 = (bf16[2,512,128]{2,1,0:T(8,128)(2,1)S(1)}, bf16[2,512,128]{2,1,0:T(8,128)(2,1)S(1)}, u32[]{:S(2)}, u32[]{:S(2)}) collective-permute-start(bf16[2,512,128]{2,1,0:T(8,128)(2,1)S(1)} %collective-permute-done.5.rest_2_), channel_id=1, source_target_pairs={{0,32},{32,0},{64,96},{96,64},{128,160},{160,128},{192,224},{224,1... | collective-permute-start | bytes 786440 | tf_op jit(solution)/shard_map/zswap/ppermute | solution.py:47
  33.2 1.0 copy-start.3
  35.2 15.7 %collective-permute-start.11 = (bf16[2,1024,128]{2,1,0:T(8,128)(2,1)S(1)}, bf16[2,1024,128]{2,1,0:T(8,128)(2,1)S(1)}, u32[]{:S(2)}, u32[]{:S(2)}) collective-permute-start(bf16[2,1024,128]{2,1,0:T(8,128)(2,1)S(1)} %get-tuple-element.33), channel_id=1, source_target_pairs={{0,16},{8,24},{16,0},{24,8},{1,17},{9,25},{17,1},{25,9},{2,18},{10... | collective-permute-start | bytes 1572872 | tf_op jit(solution)/shard_map/cache2/ppermute | solution.py:28
  51.0 18.1 %copy-start = (bf16[1024,2048]{1,0:T(8,128)(2,1)S(1)}, bf16[1024,2048]{1,0:T(8,128)(2,1)}, u32[]{:S(2)}) copy-start(bf16[1024,2048]{1,0:T(8,128)(2,1)} %w_out.3) | copy-start | bytes 12582916
  51.0 2.0 %collective-permute-start.12 = (bf16[2,1024,128]{2,1,0:T(8,128)(2,1)S(1)}, bf16[2,1024,128]{2,1,0:T(8,128)(2,1)S(1)}, u32[]{:S(2)}, u32[]{:S(2)}) collective-permute-start(bf16[2,1024,128]{2,1,0:T(8,128)(2,1)S(1)} %broadcast_add_fusion), channel_id=1, source_target_pairs={{0,32},{32,0},{64,96},{96,64},{128,160},{160,128},{192,224},{224,1... | collective-permute-start | bytes 1572872 | tf_op jit(solution)/shard_map/swap2/ppermute | solution.py:47
  56.1 9.5 %collective-permute-start.15 = (bf16[64,1024]{1,0:T(8,128)(2,1)S(1)}, bf16[64,1024]{1,0:T(8,128)(2,1)S(1)}, u32[]{:S(2)}, u32[]{:S(2)}) collective-permute-start(bf16[64,1024]{1,0:T(8,128)(2,1)S(1)} %attend_far.2.a0), channel_id=1, source_target_pairs={{0,24},{8,0},{16,8},{24,16},{1,25},{9,1},{17,9},{25,17},{2,26},{10... | collective-permute-start | bytes 393224 | tf_op jit(solution)/shard_map/gather0/ppermute | solution.py:28
  59.8 7.9 %collective-permute-start.14 = (bf16[64,1024]{1,0:T(8,128)(2,1)S(1)}, bf16[64,1024]{1,0:T(8,128)(2,1)S(1)}, u32[]{:S(2)}, u32[]{:S(2)}) collective-permute-start(bf16[64,1024]{1,0:T(8,128)(2,1)S(1)} %attend_far.2.a0), channel_id=1, source_target_pairs={{0,16},{8,24},{16,0},{24,8},{1,17},{9,25},{17,1},{25,9},{2,18},{10... | collective-permute-start | bytes 393224 | tf_op jit(solution)/shard_map/gather0/ppermute | solution.py:28
  59.8 9.3 %collective-permute-start.13 = (bf16[64,1024]{1,0:T(8,128)(2,1)S(1)}, bf16[64,1024]{1,0:T(8,128)(2,1)S(1)}, u32[]{:S(2)}, u32[]{:S(2)}) collective-permute-start(bf16[64,1024]{1,0:T(8,128)(2,1)S(1)} %attend_far.2.a0), channel_id=1, source_target_pairs={{0,8},{8,16},{16,24},{24,0},{1,9},{9,17},{17,25},{25,1},{2,10},{10... | collective-permute-start | bytes 393224 | tf_op jit(solution)/shard_map/gather0/ppermute | solution.py:28
  72.2 16.6 %collective-permute-start.16 = (bf16[2,256,256]{2,1,0:T(8,128)(2,1)S(1)}, bf16[2,256,256]{2,1,0:T(8,128)(2,1)S(1)}, u32[]{:S(2)}, u32[]{:S(2)}) collective-permute-start(bf16[2,256,256]{2,1,0:T(8,128)(2,1)S(1)} %get-tuple-element.35), channel_id=1, source_target_pairs={{0,2},{1,3},{2,4},{3,5},{4,6},{5,7},{6,0},{7,1},{8,10},{9,11},{10,... | collective-permute-start | bytes 786440 | tf_op jit(solution)/shard_map/x0/ppermute | solution.py:33
  73.7 6.2 %collective-permute-start.22 = (bf16[64,1024]{1,0:T(8,128)(2,1)S(1)}, bf16[64,1024]{1,0:T(8,128)(2,1)S(1)}, u32[]{:S(2)}, u32[]{:S(2)}) collective-permute-start(bf16[64,1024]{1,0:T(8,128)(2,1)S(1)} %attend_far.3.before.a0), channel_id=1, source_target_pairs={{0,24},{8,0},{16,8},{24,16},{1,25},{9,1},{17,9},{25,17},{2,26},{10... | collective-permute-start | bytes 393224 | tf_op jit(solution)/shard_map/gather1/ppermute | solution.py:28
  74.6 7.5 %collective-permute-start.21 = (bf16[64,1024]{1,0:T(8,128)(2,1)S(1)}, bf16[64,1024]{1,0:T(8,128)(2,1)S(1)}, u32[]{:S(2)}, u32[]{:S(2)}) collective-permute-start(bf16[64,1024]{1,0:T(8,128)(2,1)S(1)} %attend_far.3.before.a0), channel_id=1, source_target_pairs={{0,16},{8,24},{16,0},{24,8},{1,17},{9,25},{17,1},{25,9},{2,18},{10... | collective-permute-start | bytes 393224 | tf_op jit(solution)/shard_map/gather1/ppermute | solution.py:28
  74.9 8.0 %collective-permute-start.20 = (bf16[64,1024]{1,0:T(8,128)(2,1)S(1)}, bf16[64,1024]{1,0:T(8,128)(2,1)S(1)}, u32[]{:S(2)}, u32[]{:S(2)}) collective-permute-start(bf16[64,1024]{1,0:T(8,128)(2,1)S(1)} %attend_far.3.before.a0), channel_id=1, source_target_pairs={{0,8},{8,16},{16,24},{24,0},{1,9},{9,17},{17,25},{25,1},{2,10},{10... | collective-permute-start | bytes 393224 | tf_op jit(solution)/shard_map/gather1/ppermute | solution.py:28
  75.8 14.2 %collective-permute-start.17 = (bf16[2,256,256]{2,1,0:T(8,128)(2,1)S(1)}, bf16[2,256,256]{2,1,0:T(8,128)(2,1)S(1)}, u32[]{:S(2)}, u32[]{:S(2)}) collective-permute-start(bf16[2,256,256]{2,1,0:T(8,128)(2,1)S(1)} %get-tuple-element.36), channel_id=1, source_target_pairs={{0,4},{1,5},{2,6},{3,7},{4,0},{5,1},{6,2},{7,3},{8,12},{9,13},{10,... | collective-permute-start | bytes 786440 | tf_op jit(solution)/shard_map/x0/ppermute | solution.py:33
  80.0 14.6 %collective-permute-start.18 = (bf16[2,256,256]{2,1,0:T(8,128)(2,1)S(1)}, bf16[2,256,256]{2,1,0:T(8,128)(2,1)S(1)}, u32[]{:S(2)}, u32[]{:S(2)}) collective-permute-start(bf16[2,256,256]{2,1,0:T(8,128)(2,1)S(1)} %get-tuple-element.37), channel_id=1, source_target_pairs={{0,6},{1,7},{2,0},{3,1},{4,2},{5,3},{6,4},{7,5},{8,14},{9,15},{10,... | collective-permute-start | bytes 786440 | tf_op jit(solution)/shard_map/x0/ppermute | solution.py:33
  86.1 15.5 %collective-permute-start.23 = (bf16[2,256,256]{2,1,0:T(8,128)(2,1)S(1)}, bf16[2,256,256]{2,1,0:T(8,128)(2,1)S(1)}, u32[]{:S(2)}, u32[]{:S(2)}) collective-permute-start(bf16[2,256,256]{2,1,0:T(8,128)(2,1)S(1)} %get-tuple-element.42), channel_id=1, source_target_pairs={{0,2},{1,3},{2,4},{3,5},{4,6},{5,7},{6,0},{7,1},{8,10},{9,11},{10,... | collective-permute-start | bytes 786440 | tf_op jit(solution)/shard_map/x1/ppermute | solution.py:33
  87.4 14.2 %collective-permute-start.24 = (bf16[2,256,256]{2,1,0:T(8,128)(2,1)S(1)}, bf16[2,256,256]{2,1,0:T(8,128)(2,1)S(1)}, u32[]{:S(2)}, u32[]{:S(2)}) collective-permute-start(bf16[2,256,256]{2,1,0:T(8,128)(2,1)S(1)} %get-tuple-element.43), channel_id=1, source_target_pairs={{0,4},{1,5},{2,6},{3,7},{4,0},{5,1},{6,2},{7,3},{8,12},{9,13},{10,... | collective-permute-start | bytes 786440 | tf_op jit(solution)/shard_map/x1/ppermute | solution.py:33
  88.8 12.8 %collective-permute-start.25 = (bf16[2,256,256]{2,1,0:T(8,128)(2,1)S(1)}, bf16[2,256,256]{2,1,0:T(8,128)(2,1)S(1)}, u32[]{:S(2)}, u32[]{:S(2)}) collective-permute-start(bf16[2,256,256]{2,1,0:T(8,128)(2,1)S(1)} %get-tuple-element.44), channel_id=1, source_target_pairs={{0,6},{1,7},{2,0},{3,1},{4,2},{5,3},{6,4},{7,5},{8,14},{9,15},{10,... | collective-permute-start | bytes 786440 | tf_op jit(solution)/shard_map/x1/ppermute | solution.py:33
  95.2 13.1 %collective-permute-start.19 = (bf16[256,256]{1,0:T(8,128)(2,1)S(1)}, bf16[256,256]{1,0:T(8,128)(2,1)S(1)}, u32[]{:S(2)}, u32[]{:S(2)}) collective-permute-start(bf16[256,256]{1,0:T(8,128)(2,1)S(1)} %get-tuple-element.39.before), channel_id=1, source_target_pairs={{0,1},{1,0},{2,3},{3,2},{4,5},{5,4},{6,7},{7,6},{8,9},{9,8},{10,11... | collective-permute-start | bytes 393224 | tf_op jit(solution)/shard_map/z0/ppermute | solution.py:39
  102.3 11.7 %collective-permute-start.26 = (bf16[256,256]{1,0:T(8,128)(2,1)S(1)}, bf16[256,256]{1,0:T(8,128)(2,1)S(1)}, u32[]{:S(2)}, u32[]{:S(2)}) collective-permute-start(bf16[256,256]{1,0:T(8,128)(2,1)S(1)} %get-tuple-element.46), channel_id=1, source_target_pairs={{0,1},{1,0},{2,3},{3,2},{4,5},{5,4},{6,7},{7,6},{8,9},{9,8},{10,11... | collective-permute-start | bytes 393224 | tf_op jit(solution)/shard_map/z1/ppermute | solution.py:39
